TPU v7x, 32 devices: a whole 2x2x4 slice. The times are simulated.
32 devices in a mesh: shard: 4 (over y, x), ctx: 4 (over z), tp: 2 (over core).
Axes of the slice: x: 2, y: 2, z: 4, core: 2. Of those that a mesh axis runs over, the one named last changes fastest.
Arguments:
- hidden_in: bfloat16 [8192, 1024], P(('shard', 'ctx')), may hold values from -6 to 6
- cotangent: bfloat16 [8192, 1024], P(('shard', 'ctx')), may hold values from -6 to 6
- lengths: int32 [4, 3], P('shard'), may hold values from 1 to 1536, as said below
- first_gain: bfloat16 [1024], P(('shard', 'ctx')), may hold values from 0.5 to 1.5
- second_gain: bfloat16 [1024], P(('shard', 'ctx')), may hold values from 0.25 to 1.75
- mamba_gate: bfloat16 [1024, 1536], P(('shard', 'ctx'), 'tp'), may hold values from -0.1875 to 0.1875
- mamba_inner: bfloat16 [1024, 1536], P(('shard', 'ctx'), 'tp'), may hold values from -0.1875 to 0.1875
- mamba_step: bfloat16 [1024, 24], P(('shard', 'ctx'), 'tp'), may hold values from -0.1875 to 0.1875
- mamba_states: bfloat16 [1024, 256], P(('shard', 'ctx')), may hold values from -0.09375 to 0.09375
- query_weight: bfloat16 [1024, 512], P(('shard', 'ctx'), 'tp'), may hold values from -0.1875 to 0.1875
- keyval_weight: bfloat16 [1024, 256], P(('shard', 'ctx'), 'tp'), may hold values from -0.1875 to 0.1875
- mamba_output: bfloat16 [1536, 1024], P('tp', ('shard', 'ctx')), may hold values from -0.15625 to 0.15625
- attention_output: bfloat16 [512, 1024], P('tp', ('shard', 'ctx')), may hold values from -1 to 1
- gate_weight: bfloat16 [1024, 2048], P(('shard', 'ctx'), 'tp'), may hold values from -0.1875 to 0.1875
- up_weight: bfloat16 [1024, 2048], P(('shard', 'ctx'), 'tp'), may hold values from -0.1875 to 0.1875
- down_weight: bfloat16 [2048, 1024], P('tp', ('shard', 'ctx')), may hold values from -0.125 to 0.125
- decay_log: float32 [24], P('tp'), may hold values from -9 to 0
- step_bias: float32 [24], P('tp'), may hold values from -4.5 to -2
- skip_gain: float32 [24], P('tp'), may hold values from 0.5 to 1.5
- conv_inner: bfloat16 [4, 1536], P(None, 'tp'), may hold values from -3 to 3
- conv_inner_bias: bfloat16 [1536], P('tp'), may hold values from -0.5 to 0.5
- conv_states: bfloat16 [4, 256], replicated, may hold values from -3 to 3
- conv_states_bias: bfloat16 [256], replicated, may hold values from -0.19921875 to 0.19921875
Outputs:
- output: float32 [8192, 1024], P(('shard', 'ctx'))
- grad_input: float32 [8192, 1024], P(('shard', 'ctx'))
- grad_first_gain: float32 [1024], P(('shard', 'ctx'))
- grad_second_gain: float32 [1024], P(('shard', 'ctx'))
- grad_mamba_gate: float32 [1024, 1536], P(('shard', 'ctx'), 'tp')
- grad_mamba_inner: float32 [1024, 1536], P(('shard', 'ctx'), 'tp')
- grad_mamba_step: float32 [1024, 24], P(('shard', 'ctx'), 'tp')
- grad_mamba_states: float32 [1024, 256], P(('shard', 'ctx'))
- grad_query_weight: float32 [1024, 512], P(('shard', 'ctx'), 'tp')
- grad_keyval_weight: float32 [1024, 256], P(('shard', 'ctx'), 'tp')
- grad_mamba_output: float32 [1536, 1024], P('tp', ('shard', 'ctx'))
- grad_attention_output: float32 [512, 1024], P('tp', ('shard', 'ctx'))
- grad_gate_weight: float32 [1024, 2048], P(('shard', 'ctx'), 'tp')
- grad_up_weight: float32 [1024, 2048], P(('shard', 'ctx'), 'tp')
- grad_down_weight: float32 [2048, 1024], P('tp', ('shard', 'ctx'))
- grad_decay_log: float32 [24], P('tp')
- grad_step_bias: float32 [24], P('tp')
- grad_skip_gain: float32 [24], P('tp')
- grad_conv_inner: float32 [4, 1536], P(None, 'tp')
- grad_conv_inner_bias: float32 [1536], P('tp')
- grad_conv_states: float32 [4, 256], replicated
- grad_conv_states_bias: float32 [256], replicated
Inputs may be any that keep to these rules, and one draw needn't show every extreme that they name: `lengths`: in each group the first and the last document lie inside one span of 256 positions each, the middle one fills the 6 spans between them completely; every document starts at a multiple of 256.
All inputs are finite; a program needn't handle non-finite values.
Results may differ from a plain program's by a relative error of at most 0.04.
Values may be sent and summed in bfloat16 or wider, within the bound.
A program may use at most 192 MiB of HBM per device.

v0:
```python
import jax
import jax.numpy as jnp
from jax import lax
from jax.sharding import PartitionSpec as P

HEAD_DIM = 64
STATE = 128
SPAN = 256
CONV = 4
DOCS = 3


HIGHEST_PREC = lax.Precision.HIGHEST
NORM_EPS = 1e-05
MASK_FILL = -1e30


def shifted(block, axis, distance):
    devices = range(lax.axis_size(axis))
    route = [(i - distance, i) for i in devices if i - distance in devices]
    return lax.ppermute(block, axis, route)


def token_layout(seq_lens, first_row, row_count):
    span_counts = (seq_lens + SPAN - 1) // SPAN
    span_begin = jnp.cumsum(span_counts, dtype=jnp.int32) - span_counts
    row_index = first_row + jnp.arange(row_count, dtype=jnp.int32)
    row_span = row_index // SPAN
    row_doc = jnp.sum(
        (row_span[:, None] >= span_begin[None, 1:]).astype(jnp.int32), axis=1, dtype=jnp.int32
    )
    doc_onehot = row_doc[:, None] == jnp.arange(DOCS, dtype=jnp.int32)[None, :]
    doc_start = (
        jnp.sum(jnp.where(doc_onehot, span_begin[None, :], 0), axis=1, dtype=jnp.int32) * SPAN
    )
    doc_length = jnp.sum(jnp.where(doc_onehot, seq_lens[None, :], 0), axis=1, dtype=jnp.int32)
    row_pos = row_index - doc_start
    return (row_index, row_doc, row_pos, row_pos < doc_length)


def apply_rotary(values, positions, direction):
    half_dim = values.shape[-1] // 2
    frequency = 10000.0 ** (-jnp.arange(half_dim, dtype=jnp.float32) / half_dim)
    angles = positions.astype(jnp.float32)[:, None] * frequency[None, :]
    cosine = jnp.cos(angles)[:, None, :]
    sine_dir = direction * jnp.sin(angles)[:, None, :]
    leading = values[..., :half_dim]
    trailing = values[..., half_dim:]
    return jnp.concatenate(
        [leading * cosine - trailing * sine_dir, leading * sine_dir + trailing * cosine], axis=-1
    )


def times_transposed(left_mat, right_mat):
    return lax.dot_general(
        left_mat, right_mat, (((1,), (1,)), ((), ())), preferred_element_type=jnp.float32
    )


def transposed_times(left_mat, right_mat):
    return lax.dot_general(
        left_mat, right_mat, (((0,), (0,)), ((), ())), preferred_element_type=jnp.float32
    )


def norm_back(grad_out, normed, inv_scale, gain_vec):
    scaled = grad_out * gain_vec
    grad_gain = jnp.sum(grad_out * normed, axis=0)
    grad_values = inv_scale * (scaled - normed * jnp.mean(scaled * normed, axis=-1, keepdims=True))
    return (grad_gain, grad_values)


def tap_masks(positions):
    return [(positions >= lag).astype(jnp.float32)[:, None] for lag in range(CONV)]


def conv_forward(extended, kernel_f, bias_f, masks, row_count):
    total = bias_f[None, :] + jnp.zeros((row_count, extended.shape[1]), jnp.float32)
    for tap_no in range(CONV):
        total = (
            total
            + kernel_f[tap_no][None, :]
            * extended[tap_no : tap_no + row_count]
            * masks[CONV - 1 - tap_no]
        )
    return total


def conv_backward(grad_ext, extended, kernel_f, masks_ext, row_count):
    grad_values = jnp.zeros((row_count, grad_ext.shape[1]), jnp.float32)
    kernel_rows = []
    for tap_no in range(CONV):
        lag = CONV - 1 - tap_no
        masked = grad_ext * masks_ext[lag]
        grad_values = grad_values + kernel_f[tap_no][None, :] * masked[lag : lag + row_count]
        kernel_rows.append(
            jnp.sum(masked[:row_count] * extended[tap_no : tap_no + row_count], axis=0)
        )
    return (grad_values, jnp.stack(kernel_rows), jnp.sum(grad_ext[:row_count], axis=0))


def mamba_local(
    inner,
    states_in,
    intersection,
    step_raw,
    step_bias,
    decay_log,
    skip_gain,
    valid_float,
    span_keep,
    carry_in,
):
    row_total = inner.shape[0]
    head_count = step_raw.shape[1]
    span_total = row_total // SPAN
    step_size = jax.nn.softplus(step_raw + step_bias[None, :]) * valid_float[:, None]
    log_decay = -jnp.exp(decay_log)[None, :] * step_size
    inner_c = inner.reshape(span_total, SPAN, head_count, HEAD_DIM)
    b_mat = states_in[:, :STATE].reshape(span_total, SPAN, STATE)
    c_mat = states_in[:, STATE:].reshape(span_total, SPAN, STATE)
    step_c = step_size.reshape(span_total, SPAN, head_count)
    cumul = jnp.cumsum(log_decay.reshape(span_total, SPAN, head_count), axis=1)
    span_tail = cumul[:, -1]
    weights_in = jnp.exp(span_tail[:, None, :] - cumul) * step_c
    span_state = jnp.einsum(
        "cqh,cqn,cqhp->chnp", weights_in, b_mat, inner_c, precision=HIGHEST_PREC
    )
    entering = []
    running = carry_in
    for span_no in range(span_total):
        running = running * span_keep[span_no]
        entering.append(running)
        running = jnp.exp(span_tail[span_no])[:, None, None] * running + span_state[span_no]
    entering = jnp.stack(entering)
    inflow = jnp.exp(cumul)[..., None] * jnp.einsum(
        "cqn,chnp->cqhp", c_mat, entering, precision=HIGHEST_PREC
    )
    lower = jnp.arange(SPAN)[:, None] >= jnp.arange(SPAN)[None, :]
    gaps = cumul[:, :, None, :] - cumul[:, None, :, :]
    decay_mat = jnp.exp(jnp.where(lower[None, :, :, None], gaps, MASK_FILL))
    mixing = decay_mat * intersection[..., None] * step_c[:, None, :, :]
    within = jnp.einsum("cqkh,ckhp->cqhp", mixing, inner_c, precision=HIGHEST_PREC)
    result = (inflow + within + skip_gain[None, None, :, None] * inner_c).reshape(
        row_total, head_count * HEAD_DIM
    )
    total_decay = jnp.prod(span_keep[:, None] * jnp.exp(span_tail), axis=0)
    return (result, total_decay, running)


def tensor_sum(values):
    return lax.psum(values.astype(jnp.bfloat16), "tp").astype(jnp.float32)


def local(
    hidden_in,
    cotangent,
    lengths,
    first_gain,
    second_gain,
    mamba_gate,
    mamba_inner,
    mamba_step,
    mamba_states,
    query_weight,
    keyval_weight,
    mamba_output,
    attention_output,
    gate_weight,
    up_weight,
    down_weight,
    decay_log,
    step_bias,
    skip_gain,
    conv_inner,
    conv_inner_bias,
    conv_states,
    conv_states_bias,
):
    full_weights = (
        lax.all_gather(first_gain, ("shard", "ctx"), axis=0, tiled=True),
        lax.all_gather(second_gain, ("shard", "ctx"), axis=0, tiled=True),
        lax.all_gather(mamba_gate, ("shard", "ctx"), axis=0, tiled=True),
        lax.all_gather(mamba_inner, ("shard", "ctx"), axis=0, tiled=True),
        lax.all_gather(mamba_step, ("shard", "ctx"), axis=0, tiled=True),
        lax.all_gather(mamba_states, ("shard", "ctx"), axis=0, tiled=True),
        lax.all_gather(query_weight, ("shard", "ctx"), axis=0, tiled=True),
        lax.all_gather(keyval_weight, ("shard", "ctx"), axis=0, tiled=True),
        lax.all_gather(mamba_output, ("shard", "ctx"), axis=1, tiled=True),
        lax.all_gather(attention_output, ("shard", "ctx"), axis=1, tiled=True),
        lax.all_gather(gate_weight, ("shard", "ctx"), axis=0, tiled=True),
        lax.all_gather(up_weight, ("shard", "ctx"), axis=0, tiled=True),
        lax.all_gather(down_weight, ("shard", "ctx"), axis=1, tiled=True),
    )
    (
        gain_one,
        gain_two,
        mgate_full,
        inner_full,
        step_full,
        states_full,
        query_full,
        keyval_full,
        mout_full,
        aout_full,
        gate_full,
        upper_full,
        down_full,
    ) = full_weights
    seq_lens = lengths[0]
    row_total = hidden_in.shape[0]
    ctx_count = lax.axis_size("ctx")
    ctx_index = lax.axis_index("ctx")
    row_index, row_doc, row_pos, row_valid = token_layout(
        seq_lens, ctx_index * row_total, row_total
    )
    valid_float = row_valid.astype(jnp.float32)
    span_keep = (row_pos[::SPAN] != 0).astype(jnp.float32)
    hidden_f = hidden_in.astype(jnp.float32)
    gain_one_f = gain_one.astype(jnp.float32)
    gain_two_f = gain_two.astype(jnp.float32)
    inv_one = lax.rsqrt(jnp.mean(hidden_f * hidden_f, axis=-1, keepdims=True) + NORM_EPS)
    normed_one = hidden_f * inv_one
    mixer_in = (normed_one * gain_one_f).astype(jnp.bfloat16)
    q_heads = query_full.shape[1] // HEAD_DIM
    score_scale = HEAD_DIM ** (-0.5)
    query_lin = jnp.dot(mixer_in, query_full, preferred_element_type=jnp.float32)
    query_rot = apply_rotary(query_lin.reshape(row_total, q_heads, HEAD_DIM), row_pos, 1.0).astype(
        jnp.bfloat16
    )
    keyval_lin = jnp.dot(mixer_in, keyval_full, preferred_element_type=jnp.float32)
    key_rot = apply_rotary(keyval_lin[:, None, :HEAD_DIM], row_pos, 1.0)[:, 0]
    key_send = jnp.concatenate([key_rot, keyval_lin[:, HEAD_DIM:]], axis=1).astype(jnp.bfloat16)
    key_all = lax.all_gather(key_send, "ctx", axis=0, tiled=True)
    kv_width = key_all.shape[1]
    per_step = 1
    while (
        per_step * 2 <= ctx_count
        and ctx_count % (per_step * 2) == 0
        and (per_step * 2 * row_total <= 2048)
    ):
        per_step = per_step * 2
    step_rows = per_step * row_total
    key_blocks = key_all.reshape(ctx_count // per_step, step_rows, kv_width)
    block_numbers = jnp.arange(ctx_count // per_step, dtype=jnp.int32)

    def attend_block(carried, block_in):
        block_keys, block_no = block_in
        run_max, run_sum, run_acc = carried
        key_index, key_doc, key_pos, key_valid = token_layout(
            seq_lens, block_no * step_rows, step_rows
        )
        allowed = (
            (key_doc[None, :] == row_doc[:, None])
            & (key_index[None, :] <= row_index[:, None])
            & key_valid[None, :]
        )
        scores = (
            jnp.einsum(
                "qhd,kd->qhk",
                query_rot,
                block_keys[:, :HEAD_DIM],
                preferred_element_type=jnp.float32,
            )
            * score_scale
        )
        scores = jnp.where(allowed[:, None, :], scores, MASK_FILL)
        new_max = jnp.maximum(run_max, jnp.max(scores, axis=-1))
        probs = jnp.where(allowed[:, None, :], jnp.exp(scores - new_max[..., None]), 0.0)
        factor = jnp.exp(run_max - new_max)
        run_sum = run_sum * factor + jnp.sum(probs, axis=-1)
        run_acc = run_acc * factor[..., None] + jnp.einsum(
            "qhk,kd->qhd",
            probs.astype(jnp.bfloat16),
            block_keys[:, HEAD_DIM:],
            preferred_element_type=jnp.float32,
        )
        return ((new_max, run_sum, run_acc), None)

    start_fold = (
        jnp.full((row_total, q_heads), MASK_FILL, jnp.float32),
        jnp.zeros((row_total, q_heads), jnp.float32),
        jnp.zeros((row_total, q_heads, HEAD_DIM), jnp.float32),
    )
    (run_max, run_sum, run_acc), _ = lax.scan(attend_block, start_fold, (key_blocks, block_numbers))
    attn_heads = run_acc / run_sum[..., None]
    log_total = run_max + jnp.log(run_sum)
    attn_low = attn_heads.reshape(row_total, -1).astype(jnp.bfloat16)
    attn_part = jnp.dot(attn_low, aout_full, preferred_element_type=jnp.float32)
    mgate_lin = jnp.dot(mixer_in, mgate_full, preferred_element_type=jnp.float32)
    inner_pre = jnp.dot(mixer_in, inner_full, preferred_element_type=jnp.float32).astype(
        jnp.bfloat16
    )
    states_pre = jnp.dot(mixer_in, states_full, preferred_element_type=jnp.float32).astype(
        jnp.bfloat16
    )
    lead_rows = CONV - 1
    halo_inner, halo_states = shifted(
        (inner_pre[row_total - lead_rows :], states_pre[row_total - lead_rows :]), "ctx", 1
    )
    inner_ext = jnp.concatenate([halo_inner, inner_pre], axis=0).astype(jnp.float32)
    states_ext = jnp.concatenate([halo_states, states_pre], axis=0).astype(jnp.float32)
    own_masks = tap_masks(row_pos)
    conv_in_w = conv_inner.astype(jnp.float32)
    conv_st_w = conv_states.astype(jnp.float32)
    inner_conv = conv_forward(
        inner_ext, conv_in_w, conv_inner_bias.astype(jnp.float32), own_masks, row_total
    )
    states_conv = conv_forward(
        states_ext, conv_st_w, conv_states_bias.astype(jnp.float32), own_masks, row_total
    )
    sig_inner = jax.nn.sigmoid(inner_conv)
    sig_states = jax.nn.sigmoid(states_conv)
    inner_low = (inner_conv * sig_inner).astype(jnp.bfloat16)
    states_low = (states_conv * sig_states).astype(jnp.bfloat16)
    step_raw = jnp.dot(mixer_in, step_full, preferred_element_type=jnp.float32)
    inner_f = inner_low.astype(jnp.float32)
    states_f = states_low.astype(jnp.float32)
    head_local = step_raw.shape[1]
    span_total = row_total // SPAN
    b_low = states_low[:, :STATE].reshape(span_total, SPAN, STATE)
    c_low = states_low[:, STATE:].reshape(span_total, SPAN, STATE)
    intersection = jnp.einsum("cqn,ckn->cqk", c_low, b_low, preferred_element_type=jnp.float32)

    def mamba_fn(
        inner_arg, states_arg, intersection_arg, raw_arg, bias_arg, decay_arg, skip_arg, carry_arg
    ):
        return mamba_local(
            inner_arg,
            states_arg,
            intersection_arg,
            raw_arg,
            bias_arg,
            decay_arg,
            skip_arg,
            valid_float,
            span_keep,
            carry_arg,
        )

    zero_carry = jnp.zeros((head_local, STATE, HEAD_DIM), jnp.float32)
    _, dev_decay, dev_state = mamba_fn(
        inner_f, states_f, intersection, step_raw, step_bias, decay_log, skip_gain, zero_carry
    )

    def sweep_step(turn, incoming):
        return shifted(
            (dev_decay[:, None, None] * incoming + dev_state).astype(jnp.bfloat16), "ctx", 1
        ).astype(jnp.float32)

    carry_in = lax.fori_loop(0, ctx_count - 1, sweep_step, zero_carry)
    mamba_y, _, _ = mamba_fn(
        inner_f, states_f, intersection, step_raw, step_bias, decay_log, skip_gain, carry_in
    )
    sig_mgate = jax.nn.sigmoid(mgate_lin)
    silu_mgate = mgate_lin * sig_mgate
    gated_low = (mamba_y * silu_mgate).astype(jnp.bfloat16)
    mamba_part = jnp.dot(gated_low, mout_full, preferred_element_type=jnp.float32)
    resid = hidden_f + tensor_sum(attn_part + mamba_part)
    inv_two = lax.rsqrt(jnp.mean(resid * resid, axis=-1, keepdims=True) + NORM_EPS)
    normed_two = resid * inv_two
    ffn_in = (normed_two * gain_two_f).astype(jnp.bfloat16)
    gate_lin = jnp.dot(ffn_in, gate_full, preferred_element_type=jnp.float32)
    upper_lin = jnp.dot(ffn_in, upper_full, preferred_element_type=jnp.float32)
    sig_ffn = jax.nn.sigmoid(gate_lin)
    silu_ffn = gate_lin * sig_ffn
    act_low = (silu_ffn * upper_lin).astype(jnp.bfloat16)
    output = resid + tensor_sum(jnp.dot(act_low, down_full, preferred_element_type=jnp.float32))
    cot_f = cotangent.astype(jnp.float32)
    dact = times_transposed(cotangent, down_full)
    grad_down = transposed_times(act_low, cotangent)
    dgate = (dact * upper_lin * sig_ffn * (1.0 + gate_lin * (1.0 - sig_ffn))).astype(jnp.bfloat16)
    dupper = (dact * silu_ffn).astype(jnp.bfloat16)
    grad_gate = transposed_times(ffn_in, dgate)
    grad_upper = transposed_times(ffn_in, dupper)
    dffn_in = tensor_sum(times_transposed(dgate, gate_full) + times_transposed(dupper, upper_full))
    grad_gain_two, dresid_norm = norm_back(dffn_in, normed_two, inv_two, gain_two_f)
    dresid = cot_f + dresid_norm
    dmix_low = dresid.astype(jnp.bfloat16)
    dattn = times_transposed(dmix_low, aout_full).astype(jnp.bfloat16)
    grad_aout = transposed_times(attn_low, dmix_low)
    dattn_heads = dattn.reshape(row_total, q_heads, HEAD_DIM)
    delta_rows = jnp.sum(dattn_heads.astype(jnp.float32) * attn_heads, axis=-1)

    def block_grads(block_keys, block_start):
        rows_here = block_keys.shape[0]
        key_index, key_doc, key_pos, key_valid = token_layout(seq_lens, block_start, rows_here)
        allowed = (
            (key_doc[None, :] == row_doc[:, None])
            & (key_index[None, :] <= row_index[:, None])
            & key_valid[None, :]
        )
        scores = (
            jnp.einsum(
                "qhd,kd->qhk",
                query_rot,
                block_keys[:, :HEAD_DIM],
                preferred_element_type=jnp.float32,
            )
            * score_scale
        )
        probs = jnp.where(allowed[:, None, :], jnp.exp(scores - log_total[..., None]), 0.0)
        dprobs = jnp.einsum(
            "qhd,kd->qhk", dattn_heads, block_keys[:, HEAD_DIM:], preferred_element_type=jnp.float32
        )
        dscore = (probs * (dprobs - delta_rows[..., None])).astype(jnp.bfloat16)
        dq_term = (
            jnp.einsum(
                "qhk,kd->qhd", dscore, block_keys[:, :HEAD_DIM], preferred_element_type=jnp.float32
            )
            * score_scale
        )
        dkey = (
            jnp.einsum("qhk,qhd->kd", dscore, query_rot, preferred_element_type=jnp.float32)
            * score_scale
        )
        dvalue = jnp.einsum(
            "qhk,qhd->kd",
            probs.astype(jnp.bfloat16),
            dattn_heads,
            preferred_element_type=jnp.float32,
        )
        return (dq_term, jnp.concatenate([dkey, dvalue], axis=1))

    dq_zero = jnp.zeros((row_total, q_heads, HEAD_DIM), jnp.float32)

    def back_block(dq_acc, block_in):
        block_keys, block_no = block_in
        dq_term, dkv_term = block_grads(block_keys, block_no * step_rows)
        return (dq_acc + dq_term, dkv_term)

    dq_rot, dkv_terms = lax.scan(back_block, dq_zero, (key_blocks, block_numbers))
    dkv_own = lax.psum_scatter(
        dkv_terms.reshape(-1, kv_width).astype(jnp.bfloat16), "ctx", scatter_dimension=0, tiled=True
    ).astype(jnp.float32)
    dq_lin = apply_rotary(dq_rot, row_pos, -1.0).reshape(row_total, -1).astype(jnp.bfloat16)
    dkey_lin = apply_rotary(dkv_own[:, None, :HEAD_DIM], row_pos, -1.0)[:, 0]
    dkv_lin = jnp.concatenate([dkey_lin, dkv_own[:, HEAD_DIM:]], axis=1).astype(jnp.bfloat16)
    grad_query = transposed_times(mixer_in, dq_lin)
    grad_keyval = transposed_times(mixer_in, dkv_lin)
    dmixer_part = times_transposed(dq_lin, query_full) + times_transposed(dkv_lin, keyval_full)
    dgated = times_transposed(dmix_low, mout_full)
    grad_mout = transposed_times(gated_low, dmix_low)
    dmamba_y = dgated * silu_mgate
    dmgate = (dgated * mamba_y * sig_mgate * (1.0 + mgate_lin * (1.0 - sig_mgate))).astype(
        jnp.bfloat16
    )
    _, pull_carry = jax.vjp(
        lambda carry_arg: mamba_fn(
            inner_f, states_f, intersection, step_raw, step_bias, decay_log, skip_gain, carry_arg
        )[0],
        carry_in,
    )
    direct = pull_carry(dmamba_y)[0]

    def sweep_back(turn, later):
        return shifted(
            (direct + dev_decay[:, None, None] * later).astype(jnp.bfloat16), "ctx", -1
        ).astype(jnp.float32)

    adjoint_next = lax.fori_loop(0, ctx_count - 1, sweep_back, zero_carry)
    _, pull_all = jax.vjp(
        mamba_fn,
        inner_f,
        states_f,
        intersection,
        step_raw,
        step_bias,
        decay_log,
        skip_gain,
        carry_in,
    )
    dinner, dstates_direct, doverlap, dstep_raw, dbias, ddecay, dskip, _ = pull_all(
        (dmamba_y, jnp.zeros_like(dev_decay), adjoint_next)
    )
    b_f = states_f[:, :STATE].reshape(span_total, SPAN, STATE)
    c_f = states_f[:, STATE:].reshape(span_total, SPAN, STATE)
    dc_over = jnp.einsum("cqk,ckn->cqn", doverlap, b_f, precision=HIGHEST_PREC).reshape(
        row_total, STATE
    )
    db_over = jnp.einsum("cqk,cqn->ckn", doverlap, c_f, precision=HIGHEST_PREC).reshape(
        row_total, STATE
    )
    dstates = dstates_direct + jnp.concatenate([db_over, dc_over], axis=1)
    grad_inner_conv = dinner * sig_inner * (1.0 + inner_conv * (1.0 - sig_inner))
    grad_states_conv = dstates * sig_states * (1.0 + states_conv * (1.0 - sig_states))
    next_inner, next_states = shifted(
        (grad_inner_conv[:lead_rows], grad_states_conv[:lead_rows]), "ctx", -1
    )
    next_pos = token_layout(seq_lens, (ctx_index + 1) * row_total, lead_rows)[2]
    ext_masks = tap_masks(jnp.concatenate([row_pos, next_pos], axis=0))
    dinner_pre, grad_conv_inner, grad_conv_inner_bias = conv_backward(
        jnp.concatenate([grad_inner_conv, next_inner], axis=0),
        inner_ext,
        conv_in_w,
        ext_masks,
        row_total,
    )
    dstates_pre, conv_states_part, conv_sbias_part = conv_backward(
        jnp.concatenate([grad_states_conv, next_states], axis=0),
        states_ext,
        conv_st_w,
        ext_masks,
        row_total,
    )
    dinner_low = dinner_pre.astype(jnp.bfloat16)
    dstep_low = dstep_raw.astype(jnp.bfloat16)
    grad_mgate = transposed_times(mixer_in, dmgate)
    grad_inner = transposed_times(mixer_in, dinner_low)
    grad_step = transposed_times(mixer_in, dstep_low)
    dmixer_part = (
        dmixer_part
        + times_transposed(dmgate, mgate_full)
        + times_transposed(dinner_low, inner_full)
        + times_transposed(dstep_low, step_full)
    )
    dmixer_sum, dstates_sum, conv_states_grad, conv_sbias_grad = (
        lax.psum(dmixer_part.astype(jnp.bfloat16), "tp").astype(jnp.float32),
        lax.psum(dstates_pre.astype(jnp.bfloat16), "tp").astype(jnp.float32),
        lax.psum(conv_states_part.astype(jnp.bfloat16), "tp").astype(jnp.float32),
        lax.psum(conv_sbias_part.astype(jnp.bfloat16), "tp").astype(jnp.float32),
    )
    dstates_low = dstates_sum.astype(jnp.bfloat16)
    grad_states = transposed_times(mixer_in, dstates_low)
    dmixer_in = dmixer_sum + times_transposed(dstates_low, states_full)
    grad_gain_one, dhidden_norm = norm_back(dmixer_in, normed_one, inv_one, gain_one_f)
    grad_input = dresid + dhidden_norm
    grads = (
        lax.psum_scatter(grad_gain_one, ("shard", "ctx"), scatter_dimension=0, tiled=True),
        lax.psum_scatter(grad_gain_two, ("shard", "ctx"), scatter_dimension=0, tiled=True),
        lax.psum_scatter(grad_mgate, ("shard", "ctx"), scatter_dimension=0, tiled=True),
        lax.psum_scatter(grad_inner, ("shard", "ctx"), scatter_dimension=0, tiled=True),
        lax.psum_scatter(grad_step, ("shard", "ctx"), scatter_dimension=0, tiled=True),
        lax.psum_scatter(grad_states, ("shard", "ctx"), scatter_dimension=0, tiled=True),
        lax.psum_scatter(grad_query, ("shard", "ctx"), scatter_dimension=0, tiled=True),
        lax.psum_scatter(grad_keyval, ("shard", "ctx"), scatter_dimension=0, tiled=True),
        lax.psum_scatter(grad_mout, ("shard", "ctx"), scatter_dimension=1, tiled=True),
        lax.psum_scatter(grad_aout, ("shard", "ctx"), scatter_dimension=1, tiled=True),
        lax.psum_scatter(grad_gate, ("shard", "ctx"), scatter_dimension=0, tiled=True),
        lax.psum_scatter(grad_upper, ("shard", "ctx"), scatter_dimension=0, tiled=True),
        lax.psum_scatter(grad_down, ("shard", "ctx"), scatter_dimension=1, tiled=True),
    )
    head_grads = lax.psum(
        (
            ddecay,
            dbias,
            dskip,
            grad_conv_inner,
            grad_conv_inner_bias,
            conv_states_grad,
            conv_sbias_grad,
        ),
        ("shard", "ctx"),
    )
    return (output, grad_input) + tuple(grads) + tuple(head_grads)


def solution(mesh):
    in_specs = (
        P(("shard", "ctx"), None),
        P(("shard", "ctx"), None),
        P("shard", None),
        P(("shard", "ctx")),
        P(("shard", "ctx")),
        P(("shard", "ctx"), "tp"),
        P(("shard", "ctx"), "tp"),
        P(("shard", "ctx"), "tp"),
        P(("shard", "ctx"), None),
        P(("shard", "ctx"), "tp"),
        P(("shard", "ctx"), "tp"),
        P("tp", ("shard", "ctx")),
        P("tp", ("shard", "ctx")),
        P(("shard", "ctx"), "tp"),
        P(("shard", "ctx"), "tp"),
        P("tp", ("shard", "ctx")),
        P("tp"),
        P("tp"),
        P("tp"),
        P(None, "tp"),
        P("tp"),
        P(),
        P(),
    )
    out_specs = (
        P(("shard", "ctx"), None),
        P(("shard", "ctx"), None),
        P(("shard", "ctx")),
        P(("shard", "ctx")),
        P(("shard", "ctx"), "tp"),
        P(("shard", "ctx"), "tp"),
        P(("shard", "ctx"), "tp"),
        P(("shard", "ctx"), None),
        P(("shard", "ctx"), "tp"),
        P(("shard", "ctx"), "tp"),
        P("tp", ("shard", "ctx")),
        P("tp", ("shard", "ctx")),
        P(("shard", "ctx"), "tp"),
        P(("shard", "ctx"), "tp"),
        P("tp", ("shard", "ctx")),
        P("tp"),
        P("tp"),
        P("tp"),
        P(None, "tp"),
        P("tp"),
        P(),
        P(),
    )
    return jax.shard_map(local, mesh=mesh, in_specs=in_specs, out_specs=out_specs, check_vma=False)
```

profile of v0, /device:TPU:0, one launch (start us, length us, event | category | flops | bytes accessed | tf_op | source)
XLA Modules:
  0.0 1947.8 jit_solution(16975485070685186073)
XLA Ops:
  12.4 44.4 %all-reduce.14 = (bf16[1024]{0:T(1024)(128)(2,1)S(1)}, bf16[1024]{0:T(1024)(128)(2,1)}) all-reduce(bf16[1024]{0:T(1024)(128)(2,1)S(1)} %dynamic-update-slice, bf16[1024]{0:T(1024)(128)(2,1)S(1)} %dynamic-update-slice.1), channel_id=1, replica_groups=mesh['shard'=4,'ctx'=4,'tp'=2] {'shard','ctx'}, use_global_device_ids=true, to_apply=%add.9 | all-reduce | flops 2048 | bytes 8192
  58.4 42.2 %all_gather.48 = bf16[1024,256]{1,0:T(8,128)(2,1)S(1)} all-gather(bf16[64,256]{1,0:T(8,128)(2,1)} %param.35), channel_id=1, replica_groups=mesh['shard'=4,'ctx'=4,'tp'=2] {'shard','ctx'}, dimensions={0}, use_global_device_ids=true | all-gather | bytes 557056 | tf_op jit(solution)/shard_map/all_gather | solution.py:186
  102.1 4.7 collective-permute-start.2
  108.9 36.3 %all-gather = bf16[16,64,12]{1,2,0:T(8,128)(2,1)S(1)} all-gather(bf16[1,64,12]{1,2,0:T(8,128)(2,1)S(1)} %bitcast.350), channel_id=1, replica_groups=mesh['shard'=4,'ctx'=4,'tp'=2] {'shard','ctx'}, dimensions={0}, use_global_device_ids=true | all-gather | bytes 26112 | tf_op jit(solution)/shard_map/all_gather | solution.py:185
  148.8 40.6 %all_gather.44 = bf16[1024,128]{1,0:T(8,128)(2,1)S(1)} all-gather(bf16[64,128]{1,0:T(8,128)(2,1)S(1)} %copy-done.145), channel_id=1, replica_groups=mesh['shard'=4,'ctx'=4,'tp'=2] {'shard','ctx'}, dimensions={0}, use_global_device_ids=true | all-gather | bytes 278528 | tf_op jit(solution)/shard_map/all_gather | solution.py:188
  192.6 41.4 %all_gather.43 = bf16[1024,256]{1,0:T(8,128)(2,1)S(1)} all-gather(bf16[64,256]{1,0:T(8,128)(2,1)S(1)} %copy-done.119), channel_id=1, replica_groups=mesh['shard'=4,'ctx'=4,'tp'=2] {'shard','ctx'}, dimensions={0}, use_global_device_ids=true | all-gather | bytes 557056 | tf_op jit(solution)/shard_map/all_gather | solution.py:187
  234.0 43.5 %all_gather.46 = bf16[256,1024]{0,1:T(8,128)(2,1)} all-gather(bf16[256,64]{0,1:T(8,128)(2,1)S(1)} %copy-done.120), channel_id=1, replica_groups=mesh['shard'=4,'ctx'=4,'tp'=2] {'shard','ctx'}, dimensions={1}, use_global_device_ids=true | all-gather | bytes 557056 | tf_op jit(solution)/shard_map/all_gather | solution.py:190
  280.1 15.3 all_gather.45
  301.3 5.0 fusion.5
  308.0 5.5 fusion.211
  339.3 42.2 %while.6 = (s32[]{:T(128)}, f32[12,128,64]{2,1,0:T(8,128)}, f32[12]{0:T(128)S(1)}, f32[12,128,64]{2,1,0:T(8,128)}, s32[]{:T(128)}, /*index=5*/s32[]{:T(128)}) while((s32[]{:T(128)}, f32[12,128,64]{2,1,0:T(8,128)}, f32[12]{0:T(128)S(1)}, f32[12,128,64]{2,1,0:T(8,128)}, s32[]{:T(128)}, /*index=5*/s32[]{:T(128)}) %tuple.137), condition=%wide.region_14.15_spmd.clone, body=%wide.region_13.14_spmd.clone.sunk | while | flops 491523 | bytes 2359463 | solution.py:351
  341.3 4.9 collective-permute-start
  346.2 4.8 collective-permute-done
  355.3 5.1 collective-permute-start
  360.4 4.8 collective-permute-done
  369.5 5.1 collective-permute-start
  374.7 4.8 collective-permute-done
  391.4 4.8 fusion.73
  401.7 4.3 multiply_convert_fusion.6
  413.1 17.3 all-reduce.21.cloned.1.call-done
  433.9 61.4 %all-gather.16.cloned.1.call-done = bf16[1024,1024]{1,0:T(8,128)(2,1)} async-done(((bf16[64,1024]{1,0:T(8,128)(2,1)}), bf16[1024,1024]{1,0:T(8,128)(2,1)}) %all-gather.16.cloned.1.call-update) | async-done | bytes 2097168 | tf_op jit(solution)/shard_map/all_gather | solution.py:192
  495.4 4.5 fusion.218
  499.9 58.0 %all-gather.14.cloned.1.call-done = bf16[1024,1024]{1,0:T(8,128)(2,1)} async-done(((bf16[64,1024]{1,0:T(8,128)(2,1)}), bf16[1024,1024]{1,0:T(8,128)(2,1)}) %all-gather.14.cloned.1.call-update) | async-done | bytes 2097168 | tf_op jit(solution)/shard_map/all_gather | solution.py:191
  557.8 4.5 fusion.217
  562.3 58.1 %all-gather.18.cloned.1.call-done = bf16[1024,1024]{0,1:T(8,128)(2,1)} async-done(((bf16[1024,64]{0,1:T(8,128)(2,1)}), bf16[1024,1024]{0,1:T(8,128)(2,1)}) %all-gather.18.cloned.1.call-update) | async-done | bytes 2097168 | tf_op jit(solution)/shard_map/all_gather | solution.py:193
  620.4 6.3 multiply_convert_fusion.1
  636.0 4.2 convolution_convert_fusion
  640.2 9.6 all-reduce.23.cloned.1.call-done
  649.8 3.5 fusion.53
  657.7 8.9 fusion.46
  666.5 8.9 multiply_convert_fusion
  681.3 3.5 multiply_reduce_fusion.4
  697.4 8.2 fusion.23
  714.1 50.7 %while.7 = (s32[]{:T(128)}, f32[12,128,64]{2,1,0:T(8,128)}, f32[12]{0:T(128)S(1)}, f32[12,128,64]{2,1,0:T(8,128)}, s32[]{:T(128)}, /*index=5*/s32[]{:T(128)}) while((s32[]{:T(128)}, f32[12,128,64]{2,1,0:T(8,128)}, f32[12]{0:T(128)S(1)}, f32[12,128,64]{2,1,0:T(8,128)}, s32[]{:T(128)}, /*index=5*/s32[]{:T(128)}) %tuple.186), condition=%wide.region_23.24_spmd.clone, body=%wide.region_22.23_spmd.clone.sunk | while | flops 491523 | bytes 2359463 | solution.py:461
  717.5 12.2 collective-permute-done.1
  735.2 11.4 collective-permute-done.1
  752.1 10.5 collective-permute-done.1
  767.0 3.5 multiply_reduce_fusion.9
  770.5 4.7 fusion.75
  777.5 6.6 fusion.72
  801.4 5.4 reduce-window.21
  808.5 4.0 fusion.221
  823.8 3.9 add_convert_fusion
  835.0 18.0 all-reduce.25.cloned.1.call-done
  855.5 4.1 fusion.229
  859.7 3.8 fusion.225
  863.6 3.8 fusion.226
  868.6 4.6 fusion.233
  874.4 4.6 fusion.232
  879.0 4.6 fusion.231
  889.0 4.4 fusion.67
  893.5 40.6 %reduce-scatter.37.cloned.1.call-done = f32[64,12]{1,0:T(8,128)} async-done(((f32[1024,12]{1,0:T(8,128)}), f32[64,12]{1,0:T(8,128)}) %reduce-scatter.37.cloned.1.call-update) | async-done | bytes 3088
  935.7 3.7 fusion.59
  939.3 73.3 %all-reduce.13 = (f32[1024]{0:T(1024)S(1)}, f32[1024]{0:T(1024)S(1)}, f32[12]{0:T(128)}, f32[12]{0:T(128)}, f32[12]{0:T(128)}, /*index=5*/f32[4,768]{1,0:T(4,128...) all-reduce(f32[1024]{0:T(1024)S(1)} %get-tuple-element.226, ...), channel_id=3, replica_groups=mesh['shard'=4,'ctx'=4,'tp'=2] {'shard','ctx'}, use_global_device_ids=true, to_apply=%region_40.41.clone | all-reduce | flops 7204 | bytes 55072
  1013.8 4.6 fusion.58
  1018.4 70.0 %reduce-scatter.29.cloned.1.call-done = f32[256,64]{0,1:T(8,128)} async-done(((f32[256,1024]{0,1:T(8,128)}), f32[256,64]{0,1:T(8,128)}) %reduce-scatter.29.cloned.1.call-update) | async-done | bytes 65552 | tf_op jit(solution)/shard_map/reduce_scatter | solution.py:538
  1088.4 78.0 %reduce-scatter.23.cloned.1.call-done = f32[64,256]{1,0:T(8,128)} async-done(((f32[1024,256]{1,0:T(8,128)}), f32[64,256]{1,0:T(8,128)}) %reduce-scatter.23.cloned.1.call-update) | async-done | bytes 65552 | tf_op jit(solution)/shard_map/reduce_scatter | solution.py:535
  1166.4 77.9 %reduce-scatter.21.cloned.1.call-done = f32[64,256]{1,0:T(8,128)} async-done(((f32[1024,256]{1,0:T(8,128)}), f32[64,256]{1,0:T(8,128)}) %reduce-scatter.21.cloned.1.call-update) | async-done | bytes 65552 | tf_op jit(solution)/shard_map/reduce_scatter | solution.py:534
  1244.3 132.3 %reduce-scatter.27.cloned.1.call-done = f32[768,64]{0,1:T(8,128)} async-done(((f32[768,1024]{0,1:T(8,128)}), f32[768,64]{0,1:T(8,128)}) %reduce-scatter.27.cloned.1.call-update) | async-done | bytes 196624 | tf_op jit(solution)/shard_map/reduce_scatter | solution.py:537
  1376.6 135.3 %reduce-scatter.17.cloned.1.call-done = f32[64,768]{1,0:T(8,128)} async-done(((f32[1024,768]{1,0:T(8,128)}), f32[64,768]{1,0:T(8,128)}) %reduce-scatter.17.cloned.1.call-update) | async-done | bytes 196624 | tf_op jit(solution)/shard_map/reduce_scatter | solution.py:531
  1511.9 135.4 %reduce-scatter.19.cloned.1.call-done = f32[64,768]{1,0:T(8,128)} async-done(((f32[1024,768]{1,0:T(8,128)}), f32[64,768]{1,0:T(8,128)}) %reduce-scatter.19.cloned.1.call-update) | async-done | bytes 196624 | tf_op jit(solution)/shard_map/reduce_scatter | solution.py:532
  1647.3 98.5 %reduce-scatter.35.cloned.1.call-done = f32[1024,64]{0,1:T(8,128)} async-done(((f32[1024,1024]{0,1:T(8,128)}), f32[1024,64]{0,1:T(8,128)}) %reduce-scatter.35.cloned.1.call-update) | async-done | bytes 262160 | tf_op jit(solution)/shard_map/reduce_scatter | solution.py:541
  1745.8 97.4 %reduce-scatter.33.cloned.1.call-done = f32[64,1024]{1,0:T(8,128)} async-done(((f32[1024,1024]{1,0:T(8,128)}), f32[64,1024]{1,0:T(8,128)}) %reduce-scatter.33.cloned.1.call-update) | async-done | bytes 262160 | tf_op jit(solution)/shard_map/reduce_scatter | solution.py:540
  1843.2 97.5 %reduce-scatter.31.cloned.1.call-done = f32[64,1024]{1,0:T(8,128)} async-done(((f32[1024,1024]{1,0:T(8,128)}), f32[64,1024]{1,0:T(8,128)}) %reduce-scatter.31.cloned.1.call-update) | async-done | bytes 262160 | tf_op jit(solution)/shard_map/reduce_scatter | solution.py:539
  (637 shorter events, 199.3 us)
Async XLA Ops:
  7.2 93.4 %copy-start = (bf16[512,1024]{1,0:T(8,128)(2,1)S(1)}, bf16[512,1024]{1,0:T(8,128)(2,1)}, u32[]{:S(2)}) copy-start(bf16[512,1024]{1,0:T(8,128)(2,1)} %param.27) | copy-start | bytes 3145732
  7.2 309.6 %all-gather.8.cloned.1.call-start = ((), (), s32[]{:S(2)}) async-start(), calls=%async_computation.12 | async-start | bytes 1671168 | tf_op jit(solution)/shard_map/all_gather | solution.py:184
  7.9 393.8 %all-gather.10.cloned.1.call-start = ((), (), s32[]{:S(2)}) async-start(), calls=%async_computation.13 | async-start | bytes 1671168 | tf_op jit(solution)/shard_map/all_gather | solution.py:183
  8.7 397.4 %all-gather.12.cloned.1.call-start = ((), (), s32[]{:S(2)}) async-start(), calls=%async_computation.14 | async-start | bytes 1671168 | tf_op jit(solution)/shard_map/all_gather | solution.py:189
  101.0 47.8 %copy-start.145 = (bf16[64,128]{1,0:T(8,128)(2,1)S(1)}, bf16[64,128]{1,0:T(8,128)(2,1)}, u32[]{:S(2)}) copy-start(bf16[64,128]{1,0:T(8,128)(2,1)} %param.37) | copy-start | bytes 49156
  101.5 88.4 %copy-start.81 = (bf16[512,256]{1,0:T(8,128)(2,1)}, bf16[512,256]{1,0:T(8,128)(2,1)S(1)}, u32[]{:S(2)}) copy-start(bf16[512,256]{1,0:T(8,128)(2,1)S(1)} %convolution_convert_fusion.3) | copy-start | bytes 786436
  102.1 212.6 %collective-permute-start.2 = (bf16[3,256]{1,0:T(4,128)(2,1)}, bf16[3,256]{1,0:T(4,128)(2,1)}, u32[]{:S(2)}, u32[]{:S(2)}) collective-permute-start(bf16[3,256]{1,0:T(4,128)(2,1)} %slice.331), channel_id=1, source_target_pairs={{0,2},{2,4},{4,6},{1,3},{3,5},{5,7},{8,10},{10,12},{12,14},{9,11},... | collective-permute-start | bytes 4616 | tf_op jit(solution)/shard_map/ppermute | solution.py:21
  106.9 323.5 %all-reduce.21.cloned.1.call-start = ((), (), s32[]{:S(2)}) async-start(), calls=%async_computation.15 | async-start | bytes 2097152 | tf_op jit(solution)/shard_map/psum | solution.py:152
  107.0 172.8 %copy-start.164 = (f32[32]{0:T(128)}, f32[32]{0:T(128)S(1)}, u32[]{:S(2)}) copy-start(f32[32]{0:T(128)S(1)} %multiply_power_fusion) | copy-start | bytes 388
  107.2 85.3 %copy-start.171 = (s32[3]{0:T(128)}, s32[3]{0:T(128)S(1)}, u32[]{:S(2)}) copy-start(s32[3]{0:T(128)S(1)} %fusion.183) | copy-start | bytes 40
  107.9 83.8 %copy-start.174 = (s32[2]{0:T(128)}, s32[2]{0:T(128)S(1)}, u32[]{:S(2)}) copy-start(s32[2]{0:T(128)S(1)} %slice.255) | copy-start | bytes 28
  108.1 81.7 %copy-start.129 = (s32[512]{0:T(512)}, s32[512]{0:T(512)S(1)}, u32[]{:S(2)}) copy-start(s32[512]{0:T(512)S(1)} %get-tuple-element.287) | copy-start | bytes 6148
  108.1 171.7 %copy-start.118 = (f32[512]{0:T(512)}, f32[512]{0:T(512)S(1)}, u32[]{:S(2)}) copy-start(f32[512]{0:T(512)S(1)} %get-tuple-element.286) | copy-start | bytes 6148
  108.8 206.6 %copy-start.131 = (f32[512]{0:T(512)}, f32[512]{0:T(512)S(1)}, u32[]{:S(2)}) copy-start(f32[512]{0:T(512)S(1)} %get-tuple-element.340) | copy-start | bytes 6148
  108.8 206.6 %copy-start.133 = (f32[512]{0:T(512)}, f32[512]{0:T(512)S(1)}, u32[]{:S(2)}) copy-start(f32[512]{0:T(512)S(1)} %get-tuple-element.341) | copy-start | bytes 6148
  108.8 81.0 %copy-start.158 = (bf16[4,256]{1,0:T(4,128)(2,1)S(1)}, bf16[4,256]{1,0:T(4,128)(2,1)}, u32[]{:S(2)}) copy-start(bf16[4,256]{1,0:T(4,128)(2,1)} %param.48) | copy-start | bytes 6148
  108.9 83.0 %copy-start.163 = (bf16[4,768]{1,0:T(4,128)(2,1)S(1)}, bf16[4,768]{1,0:T(4,128)(2,1)}, u32[]{:S(2)}) copy-start(bf16[4,768]{1,0:T(4,128)(2,1)} %param.46) | copy-start | bytes 18436
  145.1 47.5 %copy-start.119 = (bf16[64,256]{1,0:T(8,128)(2,1)S(1)}, bf16[64,256]{1,0:T(8,128)(2,1)}, u32[]{:S(2)}) copy-start(bf16[64,256]{1,0:T(8,128)(2,1)} %param.36) | copy-start | bytes 98308
  145.3 88.7 %copy-start.120 = (bf16[256,64]{0,1:T(8,128)(2,1)S(1)}, bf16[256,64]{0,1:T(8,128)(2,1)}, u32[]{:S(2)}) copy-start(bf16[256,64]{0,1:T(8,128)(2,1)} %param.39) | copy-start | bytes 98308
  146.3 133.5 %copy-start.77 = (f32[512,12]{0,1:T(8,128)}, f32[512,12]{0,1:T(8,128)S(1)}, u32[]{:S(2)}) copy-start(f32[512,12]{0,1:T(8,128)S(1)} %get-tuple-element.291) | copy-start | bytes 73732
  148.1 130.8 %copy-start.114 = (f32[2,12]{1,0:T(2,128)}, f32[2,12]{1,0:T(2,128)S(1)}, u32[]{:S(2)}) copy-start(f32[2,12]{1,0:T(2,128)S(1)} %slice_reduce_fusion.2) | copy-start | bytes 292
  190.5 105.5 %copy-start.159 = (f32[2]{0:T(128)}, f32[2]{0:T(128)S(1)}, u32[]{:S(2)}) copy-start(f32[2]{0:T(128)S(1)} %compare_convert_fusion.3) | copy-start | bytes 28
  192.5 129.6 %copy-start.101 = (f32[768]{0:T(1024)}, f32[768]{0:T(1024)S(1)}, u32[]{:S(2)}) copy-start(f32[768]{0:T(1024)S(1)} %get-tuple-element.242) | copy-start | bytes 9220
  192.5 129.6 %copy-start.103 = (f32[768]{0:T(1024)}, f32[768]{0:T(1024)S(1)}, u32[]{:S(2)}) copy-start(f32[768]{0:T(1024)S(1)} %get-tuple-element.243) | copy-start | bytes 9220
  192.5 129.6 %copy-start.105 = (f32[768]{0:T(1024)}, f32[768]{0:T(1024)S(1)}, u32[]{:S(2)}) copy-start(f32[768]{0:T(1024)S(1)} %get-tuple-element.244) | copy-start | bytes 9220
  234.0 61.9 %copy-start.33 = (bf16[1024,256]{1,0:T(8,128)(2,1)}, bf16[1024,256]{1,0:T(8,128)(2,1)S(1)}, u32[]{:S(2)}) copy-start(bf16[1024,256]{1,0:T(8,128)(2,1)S(1)} %all_gather.43) | copy-start | bytes 1572868
  319.3 2.6 collective-permute-start.3
  341.3 9.8 collective-permute-start
  355.3 10.0 collective-permute-start
  369.5 10.0 collective-permute-start
  410.3 85.1 %all-gather.16.cloned.1.call-start = ((), (), s32[]{:S(2)}) async-start(), calls=%async_computation.17 | async-start | bytes 2228224 | tf_op jit(solution)/shard_map/all_gather | solution.py:192
  410.9 146.9 %all-gather.14.cloned.1.call-start = ((), (), s32[]{:S(2)}) async-start(), calls=%async_computation.16 | async-start | bytes 2228224 | tf_op jit(solution)/shard_map/all_gather | solution.py:191
  411.5 209.0 %all-gather.18.cloned.1.call-start = ((), (), s32[]{:S(2)}) async-start(), calls=%async_computation.18 | async-start | bytes 2228224 | tf_op jit(solution)/shard_map/all_gather | solution.py:193
  412.2 237.6 %all-reduce.23.cloned.1.call-start = ((), (), s32[]{:S(2)}) async-start(), calls=%async_computation.19 | async-start | bytes 2097152 | tf_op jit(solution)/shard_map/psum | solution.py:152
  412.5 240.8 %copy-start.92 = (f32[1024]{0:T(1024)}, f32[1024]{0:T(1024)S(1)}, u32[]{:S(2)}) copy-start(f32[1024]{0:T(1024)S(1)} %convert_element_type.277) | copy-start | bytes 12292
  432.5 220.8 %copy-start.97 = (f32[512]{0:T(512)}, f32[512]{0:T(512)S(1)}, u32[]{:S(2)}) copy-start(f32[512]{0:T(512)S(1)} %add_rsqrt_fusion) | copy-start | bytes 6148
  631.4 189.7 %reduce-scatter.15.cloned.1.call-start = ((), (), s32[]{:S(2)}) async-start(), calls=%async_computation.20 | async-start | bytes 655360 | tf_op jit(solution)/shard_map/reduce_scatter | solution.py:433
  714.1 52.8 %copy-start.162 = (f32[12]{0:T(128)S(1)}, f32[12]{0:T(128)}, u32[]{:S(2)}) copy-start(f32[12]{0:T(128)} %get-tuple-element.240) | copy-start | bytes 148
  716.2 13.5 collective-permute-start.1
  733.9 12.7 collective-permute-start.1
  750.9 11.8 collective-permute-start.1
  784.9 68.1 %all-reduce.25.cloned.1.call-start = ((), (), s32[]{:S(2)}) async-start(), calls=%async_computation.32 | async-start | bytes 4718592 | tf_op jit(solution)/shard_map/psum | solution.py:152
  790.3 23.0 %collective-permute-start.5 = (f32[3,256]{1,0:T(4,128)S(1)}, f32[3,256]{1,0:T(4,128)S(1)}, u32[]{:S(2)}, u32[]{:S(2)}) collective-permute-start(f32[3,256]{1,0:T(4,128)S(1)} %slice.370), channel_id=1, source_target_pairs={{2,0},{4,2},{6,4},{3,1},{5,3},{7,5},{10,8},{12,10},{14,12},{11,9},... | collective-permute-start | bytes 9224 | tf_op jit(solution)/shard_map/ppermute | solution.py:21
  807.1 7.9 collective-permute-start.4
  827.7 106.4 %reduce-scatter.37.cloned.1.call-start = ((), (), s32[]{:S(2)}) async-start(), calls=%async_computation.31 | async-start | bytes 557056
  829.1 189.3 %reduce-scatter.25.cloned.1.call-start = ((), (), s32[]{:S(2)}) async-start(), calls=%async_computation.25 | async-start | bytes 557056 | tf_op jit(solution)/shard_map/reduce_scatter | solution.py:536
  830.4 257.9 %reduce-scatter.29.cloned.1.call-start = ((), (), s32[]{:S(2)}) async-start(), calls=%async_computation.27 | async-start | bytes 1114112 | tf_op jit(solution)/shard_map/reduce_scatter | solution.py:538
  833.4 333.0 %reduce-scatter.23.cloned.1.call-start = ((), (), s32[]{:S(2)}) async-start(), calls=%async_computation.24 | async-start | bytes 1114112 | tf_op jit(solution)/shard_map/reduce_scatter | solution.py:535
  835.0 409.3 %reduce-scatter.21.cloned.1.call-start = ((), (), s32[]{:S(2)}) async-start(), calls=%async_computation.23 | async-start | bytes 1114112 | tf_op jit(solution)/shard_map/reduce_scatter | solution.py:534
  855.5 521.1 %reduce-scatter.27.cloned.1.call-start = ((), (), s32[]{:S(2)}) async-start(), calls=%async_computation.26 | async-start | bytes 3342336 | tf_op jit(solution)/shard_map/reduce_scatter | solution.py:537
  859.7 652.3 %reduce-scatter.17.cloned.1.call-start = ((), (), s32[]{:S(2)}) async-start(), calls=%async_computation.21 | async-start | bytes 3342336 | tf_op jit(solution)/shard_map/reduce_scatter | solution.py:531
  863.5 783.8 %reduce-scatter.19.cloned.1.call-start = ((), (), s32[]{:S(2)}) async-start(), calls=%async_computation.22 | async-start | bytes 3342336 | tf_op jit(solution)/shard_map/reduce_scatter | solution.py:532
  867.4 878.4 %reduce-scatter.35.cloned.1.call-start = ((), (), s32[]{:S(2)}) async-start(), calls=%async_computation.30 | async-start | bytes 4456448 | tf_op jit(solution)/shard_map/reduce_scatter | solution.py:541
  873.2 970.0 %reduce-scatter.33.cloned.1.call-start = ((), (), s32[]{:S(2)}) async-start(), calls=%async_computation.29 | async-start | bytes 4456448 | tf_op jit(solution)/shard_map/reduce_scatter | solution.py:540
  879.0 1061.7 %reduce-scatter.31.cloned.1.call-start = ((), (), s32[]{:S(2)}) async-start(), calls=%async_computation.28 | async-start | bytes 4456448 | tf_op jit(solution)/shard_map/reduce_scatter | solution.py:539
  889.0 46.6 %copy-start.3 = (bf16[512,1024]{1,0:T(8,128)(2,1)S(1)}, bf16[512,1024]{1,0:T(8,128)(2,1)}, u32[]{:S(2)}) copy-start(bf16[512,1024]{1,0:T(8,128)(2,1)} %param.27) | copy-start | bytes 3145732
  889.0 46.6 %copy-start.84 = (bf16[512,256]{1,0:T(8,128)(2,1)S(1)}, bf16[512,256]{1,0:T(8,128)(2,1)}, u32[]{:S(2)}) copy-start(bf16[512,256]{1,0:T(8,128)(2,1)} %get-tuple-element.281) | copy-start | bytes 786436
  889.0 46.6 %copy-start.113 = (f32[1024]{0:T(1024)S(1)}, f32[1024]{0:T(1024)}, u32[]{:S(2)}) copy-start(f32[1024]{0:T(1024)} %copy-done.112) | copy-start | bytes 12292
  889.0 46.6 %copy-start.142 = (f32[512]{0:T(512)S(1)}, f32[512]{0:T(512)}, u32[]{:S(2)}) copy-start(f32[512]{0:T(512)} %copy-done.141) | copy-start | bytes 6148
  935.6 78.2 %copy-start.6 = (bf16[512,1024]{1,0:T(8,128)(2,1)S(1)}, bf16[512,1024]{1,0:T(8,128)(2,1)}, u32[]{:S(2)}) copy-start(bf16[512,1024]{1,0:T(8,128)(2,1)} %all-reduce.21.cloned.1.call-done) | copy-start | bytes 3145732
  935.6 78.2 %copy-start.18 = (bf16[512,1024]{1,0:T(8,128)(2,1)S(1)}, bf16[512,1024]{1,0:T(8,128)(2,1)}, u32[]{:S(2)}) copy-start(bf16[512,1024]{1,0:T(8,128)(2,1)} %all-reduce.23.cloned.1.call-done) | copy-start | bytes 3145732
  935.6 78.2 %copy-start.93 = (f32[1024]{0:T(1024)S(1)}, f32[1024]{0:T(1024)}, u32[]{:S(2)}) copy-start(f32[1024]{0:T(1024)} %copy-done.92) | copy-start | bytes 12292
  935.6 78.2 %copy-start.98 = (f32[512]{0:T(512)S(1)}, f32[512]{0:T(512)}, u32[]{:S(2)}) copy-start(f32[512]{0:T(512)} %copy-done.97) | copy-start | bytes 6148
  935.7 78.2 %copy-start.140 = (f32[512]{0:T(512)S(1)}, f32[512]{0:T(512)}, u32[]{:S(2)}) copy-start(f32[512]{0:T(512)} %copy-done.139) | copy-start | bytes 6148
  (157 other events, 783.8 us)
Sparse Core Ops, SparseCore 0:
  10.9 62.0 all-gather.7
  75.8 57.3 all-gather.9
  136.0 57.1 all-gather.11
  410.4 19.8 all-reduce.20
  433.4 61.9 all-gather.15
  498.4 59.3 all-gather.13
  561.0 59.3 all-gather.17
  631.5 18.2 all-reduce.22
  785.0 21.8 reduce-scatter.14
  827.8 25.1 all-reduce.24
  855.9 78.1 reduce-scatter.36
  936.8 73.4 reduce-scatter.24
  1013.2 75.0 reduce-scatter.28
  1091.0 75.3 reduce-scatter.22
  1169.2 75.0 reduce-scatter.20
  1249.7 126.8 reduce-scatter.26
  1382.0 129.9 reduce-scatter.16
  1517.3 129.9 reduce-scatter.18
  1650.2 95.5 reduce-scatter.34
  1748.5 94.6 reduce-scatter.32
  1846.0 94.6 reduce-scatter.30
where the time goes:
time: 1950 us
  waiting for transfers between devices  1240 us (64%)
  blocking collectives  339 us (17%)
  matrix products  160 us (8%)
  other arithmetic  101 us (5%)
  local copies, waits for them, and re-layouts  60.7 us (3%)
  starting transfers between devices  29.1 us (1%)
    reduce_scatter x1, waiting for transfers between devices, local(): lax.psum_scatter(grad_inner, ('shard', 'ctx'), scatter_dimension=0, tiled...  135 us
    reduce_scatter x1, waiting for transfers between devices, local(): lax.psum_scatter(grad_mgate, ('shard', 'ctx'), scatter_dimension=0, tiled...  135 us
    reduce_scatter x1, waiting for transfers between devices, local(): lax.psum_scatter(grad_mout, ('shard', 'ctx'), scatter_dimension=1, tiled=...  132 us
    unnamed x2, blocking collectives  118 us
    reduce_scatter x1, waiting for transfers between devices, local(): lax.psum_scatter(grad_down, ('shard', 'ctx'), scatter_dimension=1, tiled=...  98.5 us
    reduce_scatter x1, waiting for transfers between devices, local(): lax.psum_scatter(grad_gate, ('shard', 'ctx'), scatter_dimension=0, tiled=...  97.5 us
    reduce_scatter x1, waiting for transfers between devices, local(): lax.psum_scatter(grad_upper, ('shard', 'ctx'), scatter_dimension=0, tiled...  97.4 us
    reduce_scatter x1, waiting for transfers between devices, local(): lax.psum_scatter(grad_query, ('shard', 'ctx'), scatter_dimension=0, tiled...  78 us
  transfers between devices with their start and end apart: 31, of which 23 were waited for; matrix products, arithmetic and copies ran while one was open for 10% of the time, Pallas kernels for 0%

commit v1 on v0

v1 whole, which is shorter than its diff:
```python
import jax
import jax.numpy as jnp
from jax import lax
from jax.sharding import PartitionSpec as P

HEAD_DIM = 64
STATE = 128
SPAN = 256
CONV = 4
DOCS = 3


NORM_EPS = 1e-05
MASK_FILL = -1e30


def shifted(block, axis, distance):
    devices = range(lax.axis_size(axis))
    route = [(i - distance, i) for i in devices if i - distance in devices]
    return lax.ppermute(block, axis, route)


def span_starts(seq_lens):
    span_counts = (seq_lens + SPAN - 1) // SPAN
    return jnp.cumsum(span_counts, dtype=jnp.int32) - span_counts


def token_layout(seq_lens, first_row, row_count):
    span_begin = span_starts(seq_lens)
    return layout_of(seq_lens, first_row + jnp.arange(row_count, dtype=jnp.int32), span_begin)


def layout_of(seq_lens, row_index, span_begin):
    row_span = row_index // SPAN
    row_doc = jnp.sum(
        (row_span[:, None] >= span_begin[None, 1:]).astype(jnp.int32), axis=1, dtype=jnp.int32
    )
    doc_onehot = row_doc[:, None] == jnp.arange(DOCS, dtype=jnp.int32)[None, :]
    doc_start = (
        jnp.sum(jnp.where(doc_onehot, span_begin[None, :], 0), axis=1, dtype=jnp.int32) * SPAN
    )
    doc_length = jnp.sum(jnp.where(doc_onehot, seq_lens[None, :], 0), axis=1, dtype=jnp.int32)
    row_pos = row_index - doc_start
    return (row_index, row_doc, row_pos, row_pos < doc_length)


def apply_rotary(values, positions, direction):
    half_dim = values.shape[-1] // 2
    frequency = 10000.0 ** (-jnp.arange(half_dim, dtype=jnp.float32) / half_dim)
    angles = positions.astype(jnp.float32)[:, None] * frequency[None, :]
    cosine = jnp.cos(angles)[:, None, :]
    sine_dir = direction * jnp.sin(angles)[:, None, :]
    leading = values[..., :half_dim]
    trailing = values[..., half_dim:]
    return jnp.concatenate(
        [leading * cosine - trailing * sine_dir, leading * sine_dir + trailing * cosine], axis=-1
    )


def times_transposed(left_mat, right_mat):
    return lax.dot_general(
        left_mat, right_mat, (((1,), (1,)), ((), ())), preferred_element_type=jnp.float32
    )


def transposed_times(left_mat, right_mat):
    return lax.dot_general(
        left_mat, right_mat, (((0,), (0,)), ((), ())), preferred_element_type=jnp.float32
    )


def norm_back(grad_out, normed, inv_scale, gain_vec):
    scaled = grad_out * gain_vec
    grad_gain = jnp.sum(grad_out * normed, axis=0)
    grad_values = inv_scale * (scaled - normed * jnp.mean(scaled * normed, axis=-1, keepdims=True))
    return (grad_gain, grad_values)


def tap_masks(positions):
    return [(positions >= lag).astype(jnp.float32)[:, None] for lag in range(CONV)]


def conv_forward(extended, kernel_f, bias_f, masks, row_count):
    total = bias_f[None, :] + jnp.zeros((row_count, extended.shape[1]), jnp.float32)
    for tap_no in range(CONV):
        total = (
            total
            + kernel_f[tap_no][None, :]
            * extended[tap_no : tap_no + row_count]
            * masks[CONV - 1 - tap_no]
        )
    return total


def conv_backward(grad_ext, extended, kernel_f, masks_ext, row_count):
    grad_values = jnp.zeros((row_count, grad_ext.shape[1]), jnp.float32)
    kernel_rows = []
    for tap_no in range(CONV):
        lag = CONV - 1 - tap_no
        masked = grad_ext * masks_ext[lag]
        grad_values = grad_values + kernel_f[tap_no][None, :] * masked[lag : lag + row_count]
        kernel_rows.append(
            jnp.sum(masked[:row_count] * extended[tap_no : tap_no + row_count], axis=0)
        )
    return (grad_values, jnp.stack(kernel_rows), jnp.sum(grad_ext[:row_count], axis=0))


def mamba_local(
    inner,
    states_in,
    intersection,
    step_raw,
    step_bias,
    decay_log,
    skip_gain,
    valid_float,
    span_keep,
    carry_in,
):
    row_total = inner.shape[0]
    head_count = step_raw.shape[1]
    span_total = row_total // SPAN
    step_size = jax.nn.softplus(step_raw + step_bias[None, :]) * valid_float[:, None]
    log_decay = -jnp.exp(decay_log)[None, :] * step_size
    inner_c = inner.reshape(span_total, SPAN, head_count, HEAD_DIM)
    b_mat = states_in[:, :STATE].reshape(span_total, SPAN, STATE)
    c_mat = states_in[:, STATE:].reshape(span_total, SPAN, STATE)
    step_c = step_size.reshape(span_total, SPAN, head_count)
    cumul = jnp.cumsum(log_decay.reshape(span_total, SPAN, head_count), axis=1)
    span_tail = cumul[:, -1]
    weights_in = jnp.exp(span_tail[:, None, :] - cumul) * step_c
    span_state = jnp.einsum(
        "cqh,cqn,cqhp->chnp", weights_in, b_mat, inner_c
    )
    entering = []
    running = carry_in
    for span_no in range(span_total):
        running = running * span_keep[span_no]
        entering.append(running)
        running = jnp.exp(span_tail[span_no])[:, None, None] * running + span_state[span_no]
    entering = jnp.stack(entering)
    inflow = jnp.exp(cumul)[..., None] * jnp.einsum(
        "cqn,chnp->cqhp", c_mat, entering
    )
    lower = jnp.arange(SPAN)[:, None] >= jnp.arange(SPAN)[None, :]
    gaps = cumul[:, :, None, :] - cumul[:, None, :, :]
    decay_mat = jnp.exp(jnp.where(lower[None, :, :, None], gaps, MASK_FILL))
    mixing = decay_mat * intersection[..., None] * step_c[:, None, :, :]
    within = jnp.einsum("cqkh,ckhp->cqhp", mixing, inner_c)
    result = (inflow + within + skip_gain[None, None, :, None] * inner_c).reshape(
        row_total, head_count * HEAD_DIM
    )
    total_decay = jnp.prod(span_keep[:, None] * jnp.exp(span_tail), axis=0)
    return (result, total_decay, running)


def tensor_sum(values):
    low = values.astype(jnp.bfloat16)
    if lax.axis_size("tp") != 2:
        return lax.psum(low, "tp").astype(jnp.float32)
    other = lax.ppermute(low, "tp", [(0, 1), (1, 0)])
    return low.astype(jnp.float32) + other.astype(jnp.float32)


def gather_state(state, decay):
    high = decay.astype(jnp.bfloat16)
    rest = (decay - high.astype(jnp.float32)).astype(jnp.bfloat16)
    heads, _, width = state.shape
    extra = jnp.stack([high, rest] + [jnp.zeros_like(high)] * 6, axis=1)
    extra = jnp.broadcast_to(extra[:, :, None], (heads, 8, width))
    packed = jnp.concatenate([state.astype(jnp.bfloat16), extra], axis=1)
    every = lax.all_gather(packed, "ctx", axis=0, tiled=False).astype(jnp.float32)
    return every[:, :, :STATE], every[:, :, STATE, 0] + every[:, :, STATE + 1, 0]


def local(
    hidden_in,
    cotangent,
    lengths,
    first_gain,
    second_gain,
    mamba_gate,
    mamba_inner,
    mamba_step,
    mamba_states,
    query_weight,
    keyval_weight,
    mamba_output,
    attention_output,
    gate_weight,
    up_weight,
    down_weight,
    decay_log,
    step_bias,
    skip_gain,
    conv_inner,
    conv_inner_bias,
    conv_states,
    conv_states_bias,
):
    both = ("shard", "ctx")
    shard_rows = mamba_gate.shape[0]
    inner_w = mamba_inner.shape[1]
    q_width = query_weight.shape[1]
    kv_width = keyval_weight.shape[1]
    head_local = mamba_step.shape[1]
    ff_w = gate_weight.shape[1]
    at_query = 2 * inner_w
    at_keyval = at_query + q_width
    at_small = at_keyval + kv_width
    at_states = at_small + 128
    small_cols = jnp.concatenate(
        [
            mamba_step,
            first_gain[:, None],
            second_gain[:, None],
            jnp.zeros((shard_rows, 128 - head_local - 2), jnp.bfloat16),
        ],
        axis=1,
    )
    mixer_shard = jnp.concatenate(
        [mamba_gate, mamba_inner, query_weight, keyval_weight, small_cols, mamba_states], axis=1
    )
    later_shard = jnp.concatenate(
        [gate_weight, up_weight, down_weight.T, attention_output.T, mamba_output.T], axis=1
    )
    mixer_w = lax.all_gather(mixer_shard, both, axis=0, tiled=True)
    mixer_w, later_shard = lax.optimization_barrier((mixer_w, later_shard))
    later_w = lax.all_gather(later_shard, both, axis=0, tiled=True)
    gate_up = later_w[:, : 2 * ff_w]
    down_t = later_w[:, 2 * ff_w : 3 * ff_w]
    out_t = later_w[:, 3 * ff_w :]
    small_w = mixer_w[:, at_small:at_states]
    states_w = mixer_w[:, at_states:]
    pick = (
        jnp.arange(8, dtype=jnp.int32)[:, None] + head_local
        == jnp.arange(128, dtype=jnp.int32)[None, :]
    ).astype(jnp.bfloat16)
    gains = times_transposed(pick, small_w)
    gain_one_f = gains[0]
    gain_two_f = gains[1]

    seq_lens = lengths[0]
    row_total, model_w = hidden_in.shape
    ctx_count = lax.axis_size("ctx")
    ctx_index = lax.axis_index("ctx")
    tp_index = lax.axis_index("tp")
    span_begin = span_starts(seq_lens)
    row_index, row_doc, row_pos, row_valid = token_layout(
        seq_lens, ctx_index * row_total, row_total
    )
    valid_float = row_valid.astype(jnp.float32)
    span_keep = (row_pos[::SPAN] != 0).astype(jnp.float32)
    hidden_f = hidden_in.astype(jnp.float32)
    inv_one = lax.rsqrt(jnp.mean(hidden_f * hidden_f, axis=-1, keepdims=True) + NORM_EPS)
    normed_one = hidden_f * inv_one
    mixer_in = (normed_one * gain_one_f).astype(jnp.bfloat16)
    q_heads = q_width // HEAD_DIM
    score_scale = HEAD_DIM ** (-0.5)
    lin = jnp.dot(mixer_in, mixer_w, preferred_element_type=jnp.float32)
    mgate_lin = lin[:, :inner_w]
    inner_pre = lin[:, inner_w:at_query].astype(jnp.bfloat16)
    query_lin = lin[:, at_query:at_keyval]
    keyval_lin = lin[:, at_keyval:at_small]
    step_raw = lin[:, at_small : at_small + head_local]
    states_pre = lin[:, at_states:].astype(jnp.bfloat16)
    lead_rows = CONV - 1
    halo = shifted(
        jnp.concatenate(
            [inner_pre[row_total - lead_rows :], states_pre[row_total - lead_rows :]], axis=1
        ),
        "ctx",
        1,
    )
    query_rot = apply_rotary(query_lin.reshape(row_total, q_heads, HEAD_DIM), row_pos, 1.0).astype(
        jnp.bfloat16
    )
    key_rot = apply_rotary(keyval_lin[:, None, :HEAD_DIM], row_pos, 1.0)[:, 0]
    key_send = jnp.concatenate([key_rot, keyval_lin[:, HEAD_DIM:]], axis=1).astype(jnp.bfloat16)
    direct_keys = ctx_count <= 4
    if direct_keys:
        step_rows = ctx_count * row_total
        key_all = jnp.concatenate(
            [key_send] + [shifted(key_send, "ctx", back) for back in range(1, ctx_count)], axis=0
        )
        key_numbers = jnp.concatenate(
            [
                (ctx_index - back) * row_total + jnp.arange(row_total, dtype=jnp.int32)
                for back in range(ctx_count)
            ]
        )
    else:
        key_all = lax.all_gather(key_send, "ctx", axis=0, tiled=True)
        step_rows = row_total * 4 if ctx_count % 4 == 0 else row_total
        key_numbers = jnp.arange(ctx_count * row_total, dtype=jnp.int32)
    key_blocks = key_all.reshape(-1, step_rows, kv_width)
    key_numbers = key_numbers.reshape(-1, step_rows)

    def allowed_pairs(key_number):
        key_index, key_doc, _, key_valid = layout_of(seq_lens, key_number, span_begin)
        return (
            (key_doc[None, :] == row_doc[:, None])
            & (key_index[None, :] <= row_index[:, None])
            & (key_valid & (key_index >= 0))[None, :]
        )

    def attend_block(carried, block_in):
        block_keys, key_number = block_in
        run_max, run_sum, run_acc = carried
        allowed = allowed_pairs(key_number)
        scores = (
            jnp.einsum(
                "qhd,kd->qhk",
                query_rot,
                block_keys[:, :HEAD_DIM],
                preferred_element_type=jnp.float32,
            )
            * score_scale
        )
        scores = jnp.where(allowed[:, None, :], scores, MASK_FILL)
        new_max = jnp.maximum(run_max, jnp.max(scores, axis=-1))
        probs = jnp.where(allowed[:, None, :], jnp.exp(scores - new_max[..., None]), 0.0)
        factor = jnp.exp(run_max - new_max)
        run_sum = run_sum * factor + jnp.sum(probs, axis=-1)
        run_acc = run_acc * factor[..., None] + jnp.einsum(
            "qhk,kd->qhd",
            probs.astype(jnp.bfloat16),
            block_keys[:, HEAD_DIM:],
            preferred_element_type=jnp.float32,
        )
        return ((new_max, run_sum, run_acc), None)

    start_fold = (
        jnp.full((row_total, q_heads), MASK_FILL, jnp.float32),
        jnp.zeros((row_total, q_heads), jnp.float32),
        jnp.zeros((row_total, q_heads, HEAD_DIM), jnp.float32),
    )
    if direct_keys:
        (run_max, run_sum, run_acc), _ = attend_block(start_fold, (key_blocks[0], key_numbers[0]))
    else:
        (run_max, run_sum, run_acc), _ = lax.scan(
            attend_block, start_fold, (key_blocks, key_numbers)
        )
    attn_heads = run_acc / run_sum[..., None]
    log_total = run_max + jnp.log(run_sum)
    attn_low = attn_heads.reshape(row_total, -1).astype(jnp.bfloat16)

    inner_ext = jnp.concatenate([halo[:, :inner_w], inner_pre], axis=0).astype(jnp.float32)
    states_ext = jnp.concatenate([halo[:, inner_w:], states_pre], axis=0).astype(jnp.float32)
    own_masks = tap_masks(row_pos)
    conv_in_w = conv_inner.astype(jnp.float32)
    conv_st_w = conv_states.astype(jnp.float32)
    inner_conv = conv_forward(
        inner_ext, conv_in_w, conv_inner_bias.astype(jnp.float32), own_masks, row_total
    )
    states_conv = conv_forward(
        states_ext, conv_st_w, conv_states_bias.astype(jnp.float32), own_masks, row_total
    )
    sig_inner = jax.nn.sigmoid(inner_conv)
    sig_states = jax.nn.sigmoid(states_conv)
    inner_low = (inner_conv * sig_inner).astype(jnp.bfloat16)
    states_low = (states_conv * sig_states).astype(jnp.bfloat16)
    inner_f = inner_low.astype(jnp.float32)
    states_f = states_low.astype(jnp.float32)
    span_total = row_total // SPAN
    b_low = states_low[:, :STATE].reshape(span_total, SPAN, STATE)
    c_low = states_low[:, STATE:].reshape(span_total, SPAN, STATE)
    intersection = jnp.einsum("cqn,ckn->cqk", c_low, b_low, preferred_element_type=jnp.float32)

    def mamba_fn(
        inner_arg, states_arg, intersection_arg, raw_arg, bias_arg, decay_arg, skip_arg, carry_arg
    ):
        return mamba_local(
            inner_arg,
            states_arg,
            intersection_arg,
            raw_arg,
            bias_arg,
            decay_arg,
            skip_arg,
            valid_float,
            span_keep,
            carry_arg,
        )

    zero_carry = jnp.zeros((head_local, STATE, HEAD_DIM), jnp.float32)
    _, dev_decay, dev_state = mamba_fn(
        inner_f, states_f, intersection, step_raw, step_bias, decay_log, skip_gain, zero_carry
    )
    every_state, every_decay = gather_state(dev_state, dev_decay)
    carry_in = zero_carry
    for owner in range(ctx_count - 1):
        carry_in = jnp.where(
            owner < ctx_index,
            every_decay[owner][:, None, None] * carry_in + every_state[owner],
            carry_in,
        )
    mamba_y, _, _ = mamba_fn(
        inner_f, states_f, intersection, step_raw, step_bias, decay_log, skip_gain, carry_in
    )
    sig_mgate = jax.nn.sigmoid(mgate_lin)
    silu_mgate = mgate_lin * sig_mgate
    gated_low = (mamba_y * silu_mgate).astype(jnp.bfloat16)
    mixed_low = jnp.concatenate([attn_low, gated_low], axis=1)
    resid = hidden_f + tensor_sum(times_transposed(mixed_low, out_t))
    inv_two = lax.rsqrt(jnp.mean(resid * resid, axis=-1, keepdims=True) + NORM_EPS)
    normed_two = resid * inv_two
    ffn_in = (normed_two * gain_two_f).astype(jnp.bfloat16)
    gate_upper = jnp.dot(ffn_in, gate_up, preferred_element_type=jnp.float32)
    gate_lin = gate_upper[:, :ff_w]
    upper_lin = gate_upper[:, ff_w:]
    sig_ffn = jax.nn.sigmoid(gate_lin)
    silu_ffn = gate_lin * sig_ffn
    act_low = (silu_ffn * upper_lin).astype(jnp.bfloat16)
    output = resid + tensor_sum(times_transposed(act_low, down_t))
    cot_f = cotangent.astype(jnp.float32)
    dact = jnp.dot(cotangent, down_t, preferred_element_type=jnp.float32)
    dgate = (dact * upper_lin * sig_ffn * (1.0 + gate_lin * (1.0 - sig_ffn))).astype(jnp.bfloat16)
    dupper = (dact * silu_ffn).astype(jnp.bfloat16)
    dgate_upper = jnp.concatenate([dgate, dupper], axis=1)
    dffn_in = tensor_sum(times_transposed(dgate_upper, gate_up))
    grad_gain_two, dresid_norm = norm_back(dffn_in, normed_two, inv_two, gain_two_f)
    dresid = cot_f + dresid_norm
    dmix_low = dresid.astype(jnp.bfloat16)
    later_grad = jnp.concatenate(
        [
            transposed_times(ffn_in, dgate_upper).astype(jnp.bfloat16),
            transposed_times(cotangent, act_low).astype(jnp.bfloat16),
            transposed_times(dmix_low, mixed_low).astype(jnp.bfloat16),
        ],
        axis=1,
    )
    later_own = lax.psum_scatter(later_grad, both, scatter_dimension=0, tiled=True)
    dmixed = jnp.dot(dmix_low, out_t, preferred_element_type=jnp.float32)
    dattn = dmixed[:, :q_width].astype(jnp.bfloat16)
    dgated = dmixed[:, q_width:]
    dattn_heads = dattn.reshape(row_total, q_heads, HEAD_DIM)
    delta_rows = jnp.sum(dattn_heads.astype(jnp.float32) * attn_heads, axis=-1)

    def back_block(dq_acc, block_in):
        block_keys, key_number = block_in
        allowed = allowed_pairs(key_number)
        scores = (
            jnp.einsum(
                "qhd,kd->qhk",
                query_rot,
                block_keys[:, :HEAD_DIM],
                preferred_element_type=jnp.float32,
            )
            * score_scale
        )
        probs = jnp.where(allowed[:, None, :], jnp.exp(scores - log_total[..., None]), 0.0)
        dprobs = jnp.einsum(
            "qhd,kd->qhk", dattn_heads, block_keys[:, HEAD_DIM:], preferred_element_type=jnp.float32
        )
        dscore = (probs * (dprobs - delta_rows[..., None])).astype(jnp.bfloat16)
        dq_term = (
            jnp.einsum(
                "qhk,kd->qhd", dscore, block_keys[:, :HEAD_DIM], preferred_element_type=jnp.float32
            )
            * score_scale
        )
        dkey = (
            jnp.einsum("qhk,qhd->kd", dscore, query_rot, preferred_element_type=jnp.float32)
            * score_scale
        )
        dvalue = jnp.einsum(
            "qhk,qhd->kd",
            probs.astype(jnp.bfloat16),
            dattn_heads,
            preferred_element_type=jnp.float32,
        )
        return (dq_acc + dq_term, jnp.concatenate([dkey, dvalue], axis=1))

    dq_zero = jnp.zeros((row_total, q_heads, HEAD_DIM), jnp.float32)
    if direct_keys:
        dq_rot, dkv_terms = back_block(dq_zero, (key_blocks[0], key_numbers[0]))
        dkv_own = dkv_terms[:row_total]
        for back in range(1, ctx_count):
            term = dkv_terms[back * row_total : (back + 1) * row_total].astype(jnp.bfloat16)
            dkv_own = dkv_own + shifted(term, "ctx", -back).astype(jnp.float32)
    else:
        dq_rot, dkv_terms = lax.scan(back_block, dq_zero, (key_blocks, key_numbers))
        dkv_own = lax.psum_scatter(
            dkv_terms.reshape(-1, kv_width).astype(jnp.bfloat16),
            "ctx",
            scatter_dimension=0,
            tiled=True,
        ).astype(jnp.float32)
    dq_lin = apply_rotary(dq_rot, row_pos, -1.0).reshape(row_total, -1).astype(jnp.bfloat16)
    dkey_lin = apply_rotary(dkv_own[:, None, :HEAD_DIM], row_pos, -1.0)[:, 0]
    dkv_lin = jnp.concatenate([dkey_lin, dkv_own[:, HEAD_DIM:]], axis=1).astype(jnp.bfloat16)
    dmamba_y = dgated * silu_mgate
    dmgate = (dgated * mamba_y * sig_mgate * (1.0 + mgate_lin * (1.0 - sig_mgate))).astype(
        jnp.bfloat16
    )
    _, pull_carry = jax.vjp(
        lambda carry_arg: mamba_fn(
            inner_f, states_f, intersection, step_raw, step_bias, decay_log, skip_gain, carry_arg
        )[0],
        carry_in,
    )
    direct = pull_carry(dmamba_y)[0]
    every_direct = lax.all_gather(direct.astype(jnp.bfloat16), "ctx", axis=0, tiled=False).astype(
        jnp.float32
    )
    adjoint_next = zero_carry
    for owner in range(ctx_count - 1, 0, -1):
        adjoint_next = jnp.where(
            owner > ctx_index,
            every_decay[owner][:, None, None] * adjoint_next + every_direct[owner],
            adjoint_next,
        )
    _, pull_all = jax.vjp(
        mamba_fn,
        inner_f,
        states_f,
        intersection,
        step_raw,
        step_bias,
        decay_log,
        skip_gain,
        carry_in,
    )
    dinner, dstates_direct, doverlap, dstep_raw, dbias, ddecay, dskip, _ = pull_all(
        (dmamba_y, jnp.zeros_like(dev_decay), adjoint_next)
    )
    b_f = states_f[:, :STATE].reshape(span_total, SPAN, STATE)
    c_f = states_f[:, STATE:].reshape(span_total, SPAN, STATE)
    dc_over = jnp.einsum("cqk,ckn->cqn", doverlap, b_f).reshape(row_total, STATE)
    db_over = jnp.einsum("cqk,cqn->ckn", doverlap, c_f).reshape(row_total, STATE)
    dstates = dstates_direct + jnp.concatenate([db_over, dc_over], axis=1)
    grad_inner_conv = dinner * sig_inner * (1.0 + inner_conv * (1.0 - sig_inner))
    grad_states_conv = dstates * sig_states * (1.0 + states_conv * (1.0 - sig_states))
    next_rows = shifted(
        jnp.concatenate([grad_inner_conv[:lead_rows], grad_states_conv[:lead_rows]], axis=1),
        "ctx",
        -1,
    )
    next_pos = token_layout(seq_lens, (ctx_index + 1) * row_total, lead_rows)[2]
    ext_masks = tap_masks(jnp.concatenate([row_pos, next_pos], axis=0))
    dstates_pre, conv_states_part, conv_sbias_part = conv_backward(
        jnp.concatenate([grad_states_conv, next_rows[:, inner_w:]], axis=0),
        states_ext,
        conv_st_w,
        ext_masks,
        row_total,
    )
    states_sum = tensor_sum(
        jnp.concatenate(
            [
                dstates_pre,
                conv_states_part,
                conv_sbias_part[None],
                jnp.zeros((3, 2 * STATE), jnp.float32),
            ],
            axis=0,
        )
    )
    dstates_low = states_sum[:row_total].astype(jnp.bfloat16)
    conv_states_grad = states_sum[row_total : row_total + CONV]
    conv_sbias_grad = states_sum[row_total + CONV]
    dinner_pre, grad_conv_inner, grad_conv_inner_bias = conv_backward(
        jnp.concatenate([grad_inner_conv, next_rows[:, :inner_w]], axis=0),
        inner_ext,
        conv_in_w,
        ext_masks,
        row_total,
    )
    dinner_low = dinner_pre.astype(jnp.bfloat16)
    dstep_low = dstep_raw.astype(jnp.bfloat16)
    mine = tp_index == 0
    dstates_half = jnp.where(mine, dstates_low[:, :STATE], dstates_low[:, STATE:])
    states_half = jnp.where(mine, states_w[:, :STATE], states_w[:, STATE:])
    dlin = jnp.concatenate([dmgate, dinner_low, dq_lin, dkv_lin, dstates_half], axis=1)
    back_w = jnp.concatenate([mixer_w[:, :at_small], states_half], axis=1)
    mixer_grad = transposed_times(mixer_in, dlin).astype(jnp.bfloat16)
    mixer_own = lax.psum_scatter(mixer_grad, both, scatter_dimension=0, tiled=True)
    grad_step_t = transposed_times(dstep_low, mixer_in)
    dmixer_in = tensor_sum(
        times_transposed(dlin, back_w) + times_transposed(dstep_low, small_w[:, :head_local])
    )
    grad_gain_one, dhidden_norm = norm_back(dmixer_in, normed_one, inv_one, gain_one_f)
    grad_input = dresid + dhidden_norm

    def wide(rows):
        return jnp.pad(rows, ((0, 0), (0, model_w - rows.shape[1])))

    small = jnp.concatenate(
        [
            grad_step_t,
            grad_gain_one[None],
            grad_gain_two[None],
            wide(grad_conv_inner),
            wide(grad_conv_inner_bias[None]),
            conv_states_grad.reshape(1, -1),
            wide(conv_sbias_grad[None]),
            wide(jnp.concatenate([ddecay, dbias, dskip])[None]),
        ],
        axis=0,
    )
    spare = -small.shape[0] % 8
    small = lax.psum(jnp.pad(small, ((0, spare), (0, 0))), both)
    own_begin = (lax.axis_index("shard") * ctx_count + ctx_index) * shard_rows
    own_cols = lax.dynamic_slice_in_dim(small[: head_local + 2], own_begin, shard_rows, 1)
    base = head_local + 2
    conv_rows = small[base : base + CONV, :inner_w]
    conv_bias_row = small[base + CONV, :inner_w]
    cstates_row = small[base + CONV + 1].reshape(CONV, 2 * STATE)
    csbias_row = small[base + CONV + 2, : 2 * STATE]
    heads_row = small[base + CONV + 3]

    later_own = later_own.astype(jnp.float32)
    at_out = 3 * ff_w
    states_own = mixer_own[:, at_small : at_small + STATE]
    states_other = lax.ppermute(states_own, "tp", [(0, 1), (1, 0)])
    grad_states = jnp.where(
        mine,
        jnp.concatenate([states_own, states_other], axis=1),
        jnp.concatenate([states_other, states_own], axis=1),
    ).astype(jnp.float32)
    mixer_own = mixer_own.astype(jnp.float32)
    return (
        output,
        grad_input,
        own_cols[head_local],
        own_cols[head_local + 1],
        mixer_own[:, :inner_w],
        mixer_own[:, inner_w:at_query],
        own_cols[:head_local].T,
        grad_states,
        mixer_own[:, at_query:at_keyval],
        mixer_own[:, at_keyval:at_small],
        later_own[:, at_out + q_width :].T,
        later_own[:, at_out : at_out + q_width].T,
        later_own[:, :ff_w],
        later_own[:, ff_w : 2 * ff_w],
        later_own[:, 2 * ff_w : at_out].T,
        heads_row[:head_local],
        heads_row[head_local : 2 * head_local],
        heads_row[2 * head_local : 3 * head_local],
        conv_rows,
        conv_bias_row,
        cstates_row,
        csbias_row,
    )


def solution(mesh):
    in_specs = (
        P(("shard", "ctx"), None),
        P(("shard", "ctx"), None),
        P("shard", None),
        P(("shard", "ctx")),
        P(("shard", "ctx")),
        P(("shard", "ctx"), "tp"),
        P(("shard", "ctx"), "tp"),
        P(("shard", "ctx"), "tp"),
        P(("shard", "ctx"), None),
        P(("shard", "ctx"), "tp"),
        P(("shard", "ctx"), "tp"),
        P("tp", ("shard", "ctx")),
        P("tp", ("shard", "ctx")),
        P(("shard", "ctx"), "tp"),
        P(("shard", "ctx"), "tp"),
        P("tp", ("shard", "ctx")),
        P("tp"),
        P("tp"),
        P("tp"),
        P(None, "tp"),
        P("tp"),
        P(),
        P(),
    )
    out_specs = (
        P(("shard", "ctx"), None),
        P(("shard", "ctx"), None),
        P(("shard", "ctx")),
        P(("shard", "ctx")),
        P(("shard", "ctx"), "tp"),
        P(("shard", "ctx"), "tp"),
        P(("shard", "ctx"), "tp"),
        P(("shard", "ctx"), None),
        P(("shard", "ctx"), "tp"),
        P(("shard", "ctx"), "tp"),
        P("tp", ("shard", "ctx")),
        P("tp", ("shard", "ctx")),
        P(("shard", "ctx"), "tp"),
        P(("shard", "ctx"), "tp"),
        P("tp", ("shard", "ctx")),
        P("tp"),
        P("tp"),
        P("tp"),
        P(None, "tp"),
        P("tp"),
        P(),
        P(),
    )
    return jax.shard_map(local, mesh=mesh, in_specs=in_specs, out_specs=out_specs, check_vma=False)
```

time: 1950 us -> 883 us (0.45)
  waiting for transfers between devices: 1240 us -> 437 us
  blocking collectives: 339 us -> 88 us
  matrix products: 160 us -> 102 us
  local copies, waits for them, and re-layouts: 60.7 us -> 92.1 us
    reduce_scatter x11 -> x2, waiting for transfers between devices: 922 us -> 267 us  [the longest x1 177 us: local(): lax.psum_scatter(later_grad, both, scatter_dimension=0, tiled=True)]
    all_gather x6 -> x2, blocking collectives: 219 us -> 88 us  [the longest x1 70.4 us: gather_state(): lax.all_gather(packed, 'ctx', axis=0, tiled=False).astype(jnp.float32)]
    unnamed x2 -> x0, blocking collectives: 118 us -> none
    all_gather x6 -> x2, waiting for transfers between devices: 178 us -> 72.1 us  [the longest x1 72.1 us: local(): mixer_w = lax.all_gather(mixer_shard, both, axis=0, tiled=True)]
    unnamed x22 -> x5, waiting for transfers between devices: 44 us -> 0.08 us
    psum x3 -> x1, waiting for transfers between devices: 44.9 us -> 84.5 us  [local(): small = lax.psum(jnp.pad(small, ((0, spare), (0, 0))), both)]
    ppermute x10 -> x8, waiting for transfers between devices: 48.8 us -> 11.3 us  [shifted(): return lax.ppermute(block, axis, route)]
    slice x1 -> x34, local copies, waits for them, and re-layouts: 0.07 us -> 24.8 us  [the longest x2 3.58 us: local(): dattn = dmixed[:, :q_width].astype(jnp.bfloat16)]
  transfers between devices with their start and end apart: 31 -> 19, of which waited for: 23 -> 6; matrix products, arithmetic and copies ran while one was open for 10% -> 21% of each run, Pallas kernels for 0% -> 0%
where the time goes in v1:
time: 883 us; the launch traced here: 873 us
  waiting for transfers between devices  437 us (49%)
  other arithmetic  119 us (13%)
  matrix products  102 us (12%)
  local copies, waits for them, and re-layouts  92.1 us (10%)
  blocking collectives  88 us (10%)
  between operations  17.7 us (2%)
  starting transfers between devices  17.2 us (2%)
    reduce_scatter x1, waiting for transfers between devices, local(): lax.psum_scatter(later_grad, both, scatter_dimension=0, tiled=True)  177 us
    reduce_scatter x1, waiting for transfers between devices, local(): lax.psum_scatter(mixer_grad, both, scatter_dimension=0, tiled=True)  89.7 us
    psum x1, waiting for transfers between devices, local(): small = lax.psum(jnp.pad(small, ((0, spare), (0, 0))), both)  84.5 us
    all_gather x1, waiting for transfers between devices, local(): mixer_w = lax.all_gather(mixer_shard, both, axis=0, tiled=True)  72.1 us
    all_gather x1, blocking collectives, gather_state(): lax.all_gather(packed, 'ctx', axis=0, tiled=False).astype(jnp.float32)  70.4 us
  transfers between devices with their start and end apart: 19, of which 6 were waited for; matrix products, arithmetic and copies ran while one was open for 21% of the time, Pallas kernels for 0%

profile of v1, /device:TPU:0, one launch (start us, length us, event | category | flops | bytes accessed | tf_op | source)
XLA Modules:
  0.0 872.5 jit_solution(645867172563554179)
XLA Ops:
  9.7 1.8 concatenate.133
  22.7 72.1 %all-gather.4.cloned.1.call-done = bf16[1024,2304]{1,0:T(8,128)(2,1)} async-done(((bf16[64,2304]{1,0:T(8,128)(2,1)}), bf16[1024,2304]{1,0:T(8,128)(2,1)}) %all-gather.4.cloned.1.call-update) | async-done | bytes 4718608 | tf_op jit(solution)/shard_map/all_gather | solution.py:227
  97.3 2.1 and_and_fusion
  100.5 6.7 fusion.255
  107.3 6.1 copy.541
  113.4 2.8 convert.79
  118.6 4.6 collective-permute-start.2
  123.3 1.9 collective-permute-start.1
  125.2 2.4 collective-permute-start
  135.7 1.7 slice.631
  137.4 11.3 %collective-permute-done.3 = bf16[3,1024]{0,1:T(8,128)(2,1)S(1)} collective-permute-done((bf16[3,1024]{0,1:T(8,128)(2,1)S(1)}, bf16[3,1024]{0,1:T(8,128)(2,1)S(1)}, u32[]{:S(2)}, u32[]{:S(2)}) %collective-permute-start.3) | collective-permute-done | bytes 6176 | tf_op jit(solution)/shard_map/ppermute | solution.py:20
  149.8 2.9 multiply_convert_fusion.5
  152.8 2.1 reshape.892
  162.6 1.7 copy.554
  169.1 70.4 %all-gather = bf16[48,136,64]{1,2,0:T(8,128)(2,1)S(1)} all-gather(bf16[12,136,64]{1,2,0:T(8,128)(2,1)S(1)} %pad_maximum_fusion.13), channel_id=2, replica_groups=mesh['shard'=4,'ctx'=4,'tp'=2] {'ctx'}, dimensions={0}, use_global_device_ids=true | all-gather | bytes 1044480 | tf_op jit(solution)/shard_map/all_gather | solution.py:172
  244.7 2.0 fusion.78
  248.1 3.4 multiply_convert_fusion.4
  252.7 3.1 select_reduce_fusion
  255.8 5.0 fusion.1
  261.9 5.6 fusion.270
  267.6 4.2 fusion.82
  272.7 2.1 collective-permute-done.4
  274.8 2.6 multiply_reduce_fusion.3
  277.4 5.3 fusion.22
  282.8 2.0 fusion.55
  284.8 3.4 fusion.92
  288.4 2.3 fusion.85
  294.1 1.8 slice_select_fusion
  295.9 3.0 multiply_reduce_fusion.1
  299.0 4.5 multiply_add_fusion
  303.5 3.6 fusion.64
  309.7 3.4 copy.626
  313.2 4.2 fusion.126
  317.3 3.7 multiply_reduce_fusion.5
  321.0 3.2 reshape.894
  324.2 6.5 fusion.25
  335.8 17.6 %all_gather.20 = bf16[4,12,128,64]{2,3,1,0:T(8,128)(2,1)S(1)} all-gather(bf16[1,12,128,64]{2,3,1,0:T(8,128)(2,1)S(1)} %fusion.148), channel_id=1, replica_groups=mesh['shard'=4,'ctx'=4,'tp'=2] {'ctx'}, dimensions={0}, use_global_device_ids=true | all-gather | bytes 983040 | tf_op jit(solution)/shard_map/all_gather | solution.py:504
  357.3 1.8 slice.978
  359.1 1.8 copy.577
  362.1 9.2 %multiply_convert_fusion = bf16[512,4,2048]{2,0,1:T(8,128)(2,1)S(1)} fusion(f32[512,4,2048]{2,0,1:T(8,128)} %copy-done.8, f32[512,4]{0,1:T(4,128)S(1)} %multiply_reduce_fusion.9, f32[512,4]{0,1:T(4,128)S(1)} %copy-done.143, pred[512,2048]{1,0:T(8,128)(4,1)} %and_and_fusion, bf16[512,4,64]{0,2,1:T(8,128)(2,1)} %bitcast.335, bf16[2048,128]{0,1:T(8,128)(2,1)} %copy-done.52), kind=kOutput, calls=%fused_computation | convolution fusion | flops 562036736 | bytes 26755072 | tf_op jit(solution)/shard_map/qhd,kd->qhk/dot_general | solution.py:453
  371.4 3.5 convolution_multiply_fusion
  374.9 2.4 fusion.45
  377.4 8.7 fusion.42
  386.1 3.1 fusion.77
  389.3 1.9 multiply_reduce_fusion.4
  391.2 3.3 fusion.155
  417.0 5.2 reduce-window.21
  426.2 2.6 fusion.257
  434.0 2.8 fusion.110
  441.1 2.0 concatenate.153
  443.1 4.6 fusion.118
  453.2 4.0 fusion.16
  462.0 2.3 fusion.203
  464.3 3.4 fusion.72
  470.1 2.7 fusion.51
  474.0 6.3 convolution_convert_fusion.1
  481.6 2.7 convert_bitcast_fusion
  484.4 2.5 convolution_convert_fusion
  488.2 3.8 pad_maximum_fusion
  492.1 4.2 fusion.50
  496.3 84.5 %all-reduce.16.cloned.1.call-done = f32[24,1024]{1,0:T(8,128)} async-done(((f32[24,1024]{1,0:T(8,128)}), f32[24,1024]{1,0:T(8,128)}) %all-reduce.16.cloned.1.call-update) | async-done | bytes 98320 | tf_op jit(solution)/shard_map/psum | solution.py:603
  589.6 89.7 %reduce-scatter.3.cloned.1.call-done = bf16[64,2048]{1,0:T(8,128)(2,1)} async-done(((bf16[1024,2048]{1,0:T(8,128)(2,1)}), bf16[64,2048]{1,0:T(8,128)(2,1)}) %reduce-scatter.3.cloned.1.call-update) | async-done | bytes 262160 | tf_op jit(solution)/shard_map/reduce_scatter | solution.py:578
  680.1 1.7 fusion.265
  685.1 177.0 %reduce-scatter.5.cloned.1.call-done = bf16[64,4096]{1,0:T(8,128)(2,1)} async-done(((bf16[1024,4096]{1,0:T(8,128)(2,1)}), bf16[64,4096]{1,0:T(8,128)(2,1)}) %reduce-scatter.5.cloned.1.call-update) | async-done | bytes 524304 | tf_op jit(solution)/shard_map/reduce_scatter | solution.py:433
  (623 shorter events, 133.9 us)
Async XLA Ops:
  7.2 88.5 %copy-start.157 = (s32[1,3]{1,0:T(1,128)S(1)}, s32[1,3]{1,0:T(1,128)}, u32[]{:S(2)}) copy-start(s32[1,3]{1,0:T(1,128)} %param.25) | copy-start | bytes 40
  7.2 88.7 %copy-start.9 = (bf16[512,1024]{1,0:T(8,128)(2,1)S(1)}, bf16[512,1024]{1,0:T(8,128)(2,1)}, u32[]{:S(2)}) copy-start(bf16[512,1024]{1,0:T(8,128)(2,1)} %param.23) | copy-start | bytes 3145732
  7.2 88.9 %copy-start.166 = (f32[12]{0:T(128)S(1)}, f32[12]{0:T(128)}, u32[]{:S(2)}) copy-start(f32[12]{0:T(128)} %param.39) | copy-start | bytes 148
  7.2 89.0 %copy-start.145 = (bf16[4,256]{1,0:T(4,128)(2,1)S(1)}, bf16[4,256]{1,0:T(4,128)(2,1)}, u32[]{:S(2)}) copy-start(bf16[4,256]{1,0:T(4,128)(2,1)} %param.44) | copy-start | bytes 6148
  7.2 87.5 %all-gather.4.cloned.1.call-start = ((), (), s32[]{:S(2)}) async-start(), calls=%async_computation.2 | async-start | bytes 5013504 | tf_op jit(solution)/shard_map/all_gather | solution.py:227
  11.5 256.1 %all-gather.6.cloned.1.call-start = ((), (), s32[]{:S(2)}) async-start(), calls=%async_computation.3 | async-start | bytes 8912896 | tf_op jit(solution)/shard_map/all_gather | solution.py:229
  13.1 83.1 %copy-start.160 = (s32[2]{0:T(128)}, s32[2]{0:T(128)S(1)}, u32[]{:S(2)}) copy-start(s32[2]{0:T(128)S(1)} %slice.482) | copy-start | bytes 28
  15.9 79.8 %copy-start.158 = (s32[3]{0:T(128)}, s32[3]{0:T(128)S(1)}, u32[]{:S(2)}) copy-start(s32[3]{0:T(128)S(1)} %fusion.233) | copy-start | bytes 40
  16.7 100.9 %copy-start.114 = (f32[512]{0:T(512)}, f32[512]{0:T(512)S(1)}, u32[]{:S(2)}) copy-start(f32[512]{0:T(512)S(1)} %get-tuple-element.68) | copy-start | bytes 6148
  17.0 114.3 %copy-start.146 = (f32[2]{0:T(128)}, f32[2]{0:T(128)S(1)}, u32[]{:S(2)}) copy-start(f32[2]{0:T(128)S(1)} %compare_convert_fusion.3) | copy-start | bytes 28
  22.7 72.1 %copy-start.65 = (bf16[64,4096]{1,0:T(8,128)(2,1)}, bf16[64,4096]{1,0:T(8,128)(2,1)S(1)}, u32[]{:S(2)}) copy-start(bf16[64,4096]{1,0:T(8,128)(2,1)S(1)} %bitcast_dynamic-update-slice_fusion.1) | copy-start | bytes 1572868
  94.8 486.0 %all-reduce.16.cloned.1.call-start = ((), (), s32[]{:S(2)}) async-start(), calls=%async_computation.4 | async-start | bytes 196608 | tf_op jit(solution)/shard_map/psum | solution.py:603
  94.9 22.8 %copy-start.148 = (f32[32]{0:T(128)}, f32[32]{0:T(128)S(1)}, u32[]{:S(2)}) copy-start(f32[32]{0:T(128)S(1)} %multiply_power_fusion) | copy-start | bytes 388
  95.7 54.1 %copy-start.98 = (f32[768]{0:T(1024)}, f32[768]{0:T(1024)S(1)}, u32[]{:S(2)}) copy-start(f32[768]{0:T(1024)S(1)} %get-tuple-element.52) | copy-start | bytes 9220
  95.7 54.1 %copy-start.100 = (f32[768]{0:T(1024)}, f32[768]{0:T(1024)S(1)}, u32[]{:S(2)}) copy-start(f32[768]{0:T(1024)S(1)} %get-tuple-element.53) | copy-start | bytes 9220
  95.7 54.1 %copy-start.102 = (f32[768]{0:T(1024)}, f32[768]{0:T(1024)S(1)}, u32[]{:S(2)}) copy-start(f32[768]{0:T(1024)S(1)} %get-tuple-element.54) | copy-start | bytes 9220
  95.7 54.1 %copy-start.104 = (f32[768]{0:T(1024)}, f32[768]{0:T(1024)S(1)}, u32[]{:S(2)}) copy-start(f32[768]{0:T(1024)S(1)} %get-tuple-element.55) | copy-start | bytes 9220
  96.2 32.8 %copy-start.156 = (f32[12]{0:T(128)}, f32[12]{0:T(128)S(1)}, u32[]{:S(2)}) copy-start(f32[12]{0:T(128)S(1)} %exponential_negate_fusion) | copy-start | bytes 148
  96.2 60.8 %copy-start.130 = (f32[1,256]{1,0:T(1,128)}, f32[1,256]{1,0:T(1,128)S(1)}, u32[]{:S(2)}) copy-start(f32[1,256]{1,0:T(1,128)S(1)} %get-tuple-element.139) | copy-start | bytes 3076
  96.3 60.8 %copy-start.132 = (f32[1,256]{1,0:T(1,128)}, f32[1,256]{1,0:T(1,128)S(1)}, u32[]{:S(2)}) copy-start(f32[1,256]{1,0:T(1,128)S(1)} %get-tuple-element.140) | copy-start | bytes 3076
  96.3 60.8 %copy-start.134 = (f32[1,256]{1,0:T(1,128)}, f32[1,256]{1,0:T(1,128)S(1)}, u32[]{:S(2)}) copy-start(f32[1,256]{1,0:T(1,128)S(1)} %get-tuple-element.141) | copy-start | bytes 3076
  96.3 60.8 %copy-start.136 = (f32[1,256]{1,0:T(1,128)}, f32[1,256]{1,0:T(1,128)S(1)}, u32[]{:S(2)}) copy-start(f32[1,256]{1,0:T(1,128)S(1)} %get-tuple-element.142) | copy-start | bytes 3076
  96.3 32.7 %copy-start.121 = (f32[512]{0:T(512)}, f32[512]{0:T(512)S(1)}, u32[]{:S(2)}) copy-start(f32[512]{0:T(512)S(1)} %get-tuple-element.134) | copy-start | bytes 6148
  97.3 37.1 %copy-start.70 = (f32[512,32]{0,1:T(8,128)}, f32[512,32]{0,1:T(8,128)S(1)}, u32[]{:S(2)}) copy-start(f32[512,32]{0,1:T(8,128)S(1)} %get-tuple-element.129) | copy-start | bytes 196612
  100.5 198.4 %copy-start.96 = (f32[1,1024]{1,0:T(1,128)}, f32[1,1024]{1,0:T(1,128)S(1)}, u32[]{:S(2)}) copy-start(f32[1,1024]{1,0:T(1,128)S(1)} %get-tuple-element.118) | copy-start | bytes 12292
  107.2 21.8 %slice-start.1 = ((s8[4718592]{0:T(1024)(128)(4,1)}), s8[524288]{0:T(1024)(128)(4,1)S(1)}, s32[]{:S(2)}) async-start(s8[4718592]{0:T(1024)(128)(4,1)} %bitcast.319), calls=%async_computation.8 | async-start | bytes 1048576
  113.4 15.7 %slice-start.2 = ((s8[4718592]{0:T(1024)(128)(4,1)}), s8[4194304]{0:T(1024)(128)(4,1)S(1)}, s32[]{:S(2)}) async-start(s8[4718592]{0:T(1024)(128)(4,1)} %bitcast.319), calls=%async_computation.9 | async-start | bytes 8388608
  116.2 13.0 %copy-start.28 = (bf16[512,2304]{0,1:T(8,128)(2,1)}, bf16[512,2304]{0,1:T(8,128)(2,1)S(1)}, u32[]{:S(2)}) copy-start(bf16[512,2304]{0,1:T(8,128)(2,1)S(1)} %convert.79) | copy-start | bytes 7077892
  116.5 14.6 %copy-start.72 = (bf16[512,64]{0,1:T(8,128)(2,1)}, bf16[512,64]{0,1:T(8,128)(2,1)S(1)}, u32[]{:S(2)}) copy-start(bf16[512,64]{0,1:T(8,128)(2,1)S(1)} %slice.621) | copy-start | bytes 196612
  116.5 15.6 %slice-start.3 = ((f32[512,2304]{1,0:T(8,128)}), f32[512,256]{1,0:T(8,128)S(1)}, s32[]{:S(2)}) async-start(f32[512,2304]{1,0:T(8,128)} %fusion.255), calls=%async_computation.10 | async-start | bytes 1048576 | tf_op jit(solution)/shard_map/slice | solution.py:263
  118.0 14.4 %copy-start.74 = (bf16[512,64]{0,1:T(8,128)(2,1)}, bf16[512,64]{0,1:T(8,128)(2,1)S(1)}, u32[]{:S(2)}) copy-start(bf16[512,64]{0,1:T(8,128)(2,1)S(1)} %maximum_bitcast_fusion) | copy-start | bytes 196612
  118.6 132.9 %collective-permute-start.2 = (bf16[512,128]{0,1:T(8,128)(2,1)}, bf16[512,128]{0,1:T(8,128)(2,1)}, u32[]{:S(2)}, u32[]{:S(2)}) collective-permute-start(bf16[512,128]{0,1:T(8,128)(2,1)} %pad_maximum_fusion.19), channel_id=1, source_target_pairs={{0,6},{1,7},{8,14},{9,15},{16,22},{17,23},{24,30},{25,31}} | collective-permute-start | bytes 393224 | tf_op jit(solution)/shard_map/ppermute | solution.py:20
  123.3 128.3 %collective-permute-start.1 = (bf16[512,128]{0,1:T(8,128)(2,1)}, bf16[512,128]{0,1:T(8,128)(2,1)}, u32[]{:S(2)}, u32[]{:S(2)}) collective-permute-start(bf16[512,128]{0,1:T(8,128)(2,1)} %pad_maximum_fusion.19), channel_id=1, source_target_pairs={{0,4},{2,6},{1,5},{3,7},{8,12},{10,14},{9,13},{11,15},{16,20},{18,... | collective-permute-start | bytes 393224 | tf_op jit(solution)/shard_map/ppermute | solution.py:20
  125.2 126.4 %collective-permute-start = (bf16[512,128]{0,1:T(8,128)(2,1)}, bf16[512,128]{0,1:T(8,128)(2,1)}, u32[]{:S(2)}, u32[]{:S(2)}) collective-permute-start(bf16[512,128]{0,1:T(8,128)(2,1)} %pad_maximum_fusion.19), channel_id=1, source_target_pairs={{0,2},{2,4},{4,6},{1,3},{3,5},{5,7},{8,10},{10,12},{12,14},{9,11},... | collective-permute-start | bytes 393224 | tf_op jit(solution)/shard_map/ppermute | solution.py:20
  127.7 20.9 %collective-permute-start.3 = (bf16[3,1024]{0,1:T(8,128)(2,1)S(1)}, bf16[3,1024]{0,1:T(8,128)(2,1)S(1)}, u32[]{:S(2)}, u32[]{:S(2)}) collective-permute-start(bf16[3,1024]{0,1:T(8,128)(2,1)S(1)} %pad_maximum_fusion.15), channel_id=1, source_target_pairs={{0,2},{2,4},{4,6},{1,3},{3,5},{5,7},{8,10},{10,12},{12,14},{9,11},... | collective-permute-start | bytes 18440 | tf_op jit(solution)/shard_map/ppermute | solution.py:20
  131.2 282.0 %copy-start.113 = (f32[2,12]{1,0:T(2,128)}, f32[2,12]{1,0:T(2,128)S(1)}, u32[]{:S(2)}) copy-start(f32[2,12]{1,0:T(2,128)S(1)} %slice_reduce_fusion.2) | copy-start | bytes 292
  132.1 17.3 %slice-start.4 = ((bf16[512,2304]{0,1:T(8,128)(2,1)}), bf16[512,768]{0,1:T(8,128)(2,1)S(1)}, s32[]{:S(2)}) async-start(bf16[512,2304]{0,1:T(8,128)(2,1)} %copy-done.28), calls=%async_computation.11 | async-start | bytes 1572864 | tf_op jit(solution)/shard_map/slice | solution.py:262
  133.0 15.6 %copy-start.127 = (f32[12]{0:T(128)}, f32[12]{0:T(128)S(1)}, u32[]{:S(2)}) copy-start(f32[12]{0:T(128)S(1)} %get-tuple-element.47) | copy-start | bytes 148
  167.5 73.5 %copy-start.35 = (f32[2,12,128,64]{2,3,1,0:T(8,128)}, f32[2,12,128,64]{2,3,1,0:T(8,128)S(1)}, u32[]{:S(2)}) copy-start(f32[2,12,128,64]{2,3,1,0:T(8,128)S(1)} %fusion.105) | copy-start | bytes 2359300
  271.8 3.0 collective-permute-start.4
  277.4 21.6 %copy-start.119 = (f32[512]{0:T(512)}, f32[512]{0:T(512)S(1)}, u32[]{:S(2)}) copy-start(f32[512]{0:T(512)S(1)} %add_rsqrt_fusion) | copy-start | bytes 6148
  288.2 7.7 collective-permute-start.6
  290.7 8.3 collective-permute-start.5
  334.2 19.3 %copy-start.21 = (f32[2,12,128,64]{2,3,1,0:T(8,128)}, f32[2,12,128,64]{2,3,1,0:T(8,128)S(1)}, u32[]{:S(2)}) copy-start(f32[2,12,128,64]{2,3,1,0:T(8,128)S(1)} %fusion.102) | copy-start | bytes 2359300
  334.2 19.3 %copy-start.126 = (f32[12]{0:T(128)S(1)}, f32[12]{0:T(128)}, u32[]{:S(2)}) copy-start(f32[12]{0:T(128)} %get-tuple-element.46) | copy-start | bytes 148
  334.2 19.3 %copy-start.139 = (f32[12]{0:T(128)S(1)}, f32[12]{0:T(128)}, u32[]{:S(2)}) copy-start(f32[12]{0:T(128)} %copy-done.138) | copy-start | bytes 148
  334.2 19.3 %copy-start.141 = (f32[12]{0:T(128)S(1)}, f32[12]{0:T(128)}, u32[]{:S(2)}) copy-start(f32[12]{0:T(128)} %copy-done.140) | copy-start | bytes 148
  334.2 19.3 %copy-start.150 = (f32[12]{0:T(128)S(1)}, f32[12]{0:T(128)}, u32[]{:S(2)}) copy-start(f32[12]{0:T(128)} %get-tuple-element.48) | copy-start | bytes 148
  405.2 24.3 %collective-permute-start.7 = (f32[3,1024]{0,1:T(8,128)}, f32[3,1024]{0,1:T(8,128)}, u32[]{:S(2)}, u32[]{:S(2)}) collective-permute-start(f32[3,1024]{0,1:T(8,128)} %pad_maximum_fusion.12), channel_id=1, source_target_pairs={{2,0},{4,2},{6,4},{3,1},{5,3},{7,5},{10,8},{12,10},{14,12},{11,9},... | collective-permute-start | bytes 36872 | tf_op jit(solution)/shard_map/ppermute | solution.py:20
  406.8 18.3 %copy-start.71 = (f32[512,32]{0,1:T(8,128)S(1)}, f32[512,32]{0,1:T(8,128)}, u32[]{:S(2)}) copy-start(f32[512,32]{0,1:T(8,128)} %copy-done.70) | copy-start | bytes 196612
  407.5 18.6 %copy-start.38 = (f32[512,12]{1,0:T(8,128)S(1)}, f32[512,12]{1,0:T(8,128)}, u32[]{:S(2)}) copy-start(f32[512,12]{1,0:T(8,128)} %copy-done.37) | copy-start | bytes 73732
  407.5 41.0 %collective-permute-start.10 = (bf16[512,128]{0,1:T(8,128)(2,1)}, bf16[512,128]{0,1:T(8,128)(2,1)}, u32[]{:S(2)}, u32[]{:S(2)}) collective-permute-start(bf16[512,128]{0,1:T(8,128)(2,1)} %get-tuple-element.100), channel_id=1, source_target_pairs={{6,0},{7,1},{14,8},{15,9},{22,16},{23,17},{30,24},{31,25}} | collective-permute-start | bytes 393224 | tf_op jit(solution)/shard_map/ppermute | solution.py:20
  408.9 39.6 %collective-permute-start.9 = (bf16[512,128]{0,1:T(8,128)(2,1)}, bf16[512,128]{0,1:T(8,128)(2,1)}, u32[]{:S(2)}, u32[]{:S(2)}) collective-permute-start(bf16[512,128]{0,1:T(8,128)(2,1)} %get-tuple-element.101), channel_id=1, source_target_pairs={{4,0},{6,2},{5,1},{7,3},{12,8},{14,10},{13,9},{15,11},{20,16},{22,... | collective-permute-start | bytes 393224 | tf_op jit(solution)/shard_map/ppermute | solution.py:20
  410.2 38.3 %collective-permute-start.8 = (bf16[512,128]{0,1:T(8,128)(2,1)}, bf16[512,128]{0,1:T(8,128)(2,1)}, u32[]{:S(2)}, u32[]{:S(2)}) collective-permute-start(bf16[512,128]{0,1:T(8,128)(2,1)} %get-tuple-element.99), channel_id=1, source_target_pairs={{2,0},{4,2},{6,4},{3,1},{5,3},{7,5},{10,8},{12,10},{14,12},{11,9},... | collective-permute-start | bytes 393224 | tf_op jit(solution)/shard_map/ppermute | solution.py:20
  413.3 17.2 %copy-start.18 = (f32[512,256]{0,1:T(8,128)S(1)}, f32[512,256]{0,1:T(8,128)}, u32[]{:S(2)}) copy-start(f32[512,256]{0,1:T(8,128)} %copy-done.17) | copy-start | bytes 1572868
  416.2 14.2 %copy-start.105 = (f32[515]{0:T(1024)S(1)}, f32[515]{0:T(1024)}, u32[]{:S(2)}) copy-start(f32[515]{0:T(1024)} %get-tuple-element.131) | copy-start | bytes 6184
  416.2 14.2 %copy-start.107 = (f32[515]{0:T(1024)S(1)}, f32[515]{0:T(1024)}, u32[]{:S(2)}) copy-start(f32[515]{0:T(1024)} %get-tuple-element.132) | copy-start | bytes 6184
  416.2 14.2 %copy-start.109 = (f32[515]{0:T(1024)S(1)}, f32[515]{0:T(1024)}, u32[]{:S(2)}) copy-start(f32[515]{0:T(1024)} %get-tuple-element.133) | copy-start | bytes 6184
  443.1 8.4 collective-permute-start.11
  443.1 14.1 %slice-start.5 = ((s8[4718592]{0:T(1024)(128)(4,1)}), s8[4194304]{0:T(1024)(128)(4,1)S(1)}, s32[]{:S(2)}) async-start(s8[4718592]{0:T(1024)(128)(4,1)} %bitcast.327), calls=%async_computation.12 | async-start | bytes 8388608
  458.7 11.4 %collective-permute-start.12 = (bf16[512,1024]{1,0:T(8,128)(2,1)}, bf16[512,1024]{1,0:T(8,128)(2,1)}, u32[]{:S(2)}, u32[]{:S(2)}) collective-permute-start(bf16[512,1024]{1,0:T(8,128)(2,1)} %add_convert_fusion), channel_id=1, source_target_pairs={{0,1},{1,0},{2,3},{3,2},{4,5},{5,4},{6,7},{7,6},{8,9},{9,8},{10,11... | collective-permute-start | bytes 3145736 | tf_op jit(solution)/shard_map/ppermute | solution.py:161
  473.7 205.6 %reduce-scatter.3.cloned.1.call-start = ((), (), s32[]{:S(2)}) async-start(), calls=%async_computation.5 | async-start | bytes 4456448 | tf_op jit(solution)/shard_map/reduce_scatter | solution.py:578
  480.4 381.7 %reduce-scatter.5.cloned.1.call-start = ((), (), s32[]{:S(2)}) async-start(), calls=%async_computation.6 | async-start | bytes 8912896 | tf_op jit(solution)/shard_map/reduce_scatter | solution.py:433
  680.1 4.4 collective-permute-start.13
  (140 other events, 621.6 us)
Sparse Core Ops, SparseCore 0:
  11.6 83.1 all-gather.3
  98.1 145.0 all-gather.5
  473.8 106.9 all-reduce.15
  582.9 96.3 reduce-scatter.2
  681.5 180.5 reduce-scatter.4

commit v2 on v1

--- a/solution.py
+++ b/solution.py
@@ -162,15 +162,42 @@
     return low.astype(jnp.float32) + other.astype(jnp.float32)
 
 
-def gather_state(state, decay):
+def far_states(state, decay, direction):
+    heads, _, width = state.shape
     high = decay.astype(jnp.bfloat16)
     rest = (decay - high.astype(jnp.float32)).astype(jnp.bfloat16)
-    heads, _, width = state.shape
     extra = jnp.stack([high, rest] + [jnp.zeros_like(high)] * 6, axis=1)
     extra = jnp.broadcast_to(extra[:, :, None], (heads, 8, width))
     packed = jnp.concatenate([state.astype(jnp.bfloat16), extra], axis=1)
+    count = lax.axis_size("ctx")
+    total = jnp.zeros(state.shape, jnp.float32)
+    if count <= 4:
+        for distance in range(count - 1, 0, -1):
+            got = shifted(packed, "ctx", direction * distance).astype(jnp.float32)
+            factor = got[:, STATE, 0] + got[:, STATE + 1, 0]
+            total = factor[:, None, None] * total + got[:, :STATE]
+        return total
+    index = lax.axis_index("ctx")
     every = lax.all_gather(packed, "ctx", axis=0, tiled=False).astype(jnp.float32)
-    return every[:, :, :STATE], every[:, :, STATE, 0] + every[:, :, STATE + 1, 0]
+    for owner in range(count)[::direction]:
+        factor = every[owner, :, STATE, 0] + every[owner, :, STATE + 1, 0]
+        total = jnp.where(
+            (index - owner) * direction > 0,
+            factor[:, None, None] * total + every[owner, :, :STATE],
+            total,
+        )
+    return total
+
+
+def doubling_sum(values, axis):
+    count = lax.axis_size(axis)
+    if count & (count - 1):
+        return lax.psum(values, axis)
+    step = 1
+    while step < count:
+        values = values + lax.ppermute(values, axis, [(i, i ^ step) for i in range(count)])
+        step = step * 2
+    return values
 
 
 def local(
@@ -205,10 +232,9 @@
     kv_width = keyval_weight.shape[1]
     head_local = mamba_step.shape[1]
     ff_w = gate_weight.shape[1]
-    at_query = 2 * inner_w
-    at_keyval = at_query + q_width
+    at_states = inner_w
+    at_keyval = at_states + 2 * STATE
     at_small = at_keyval + kv_width
-    at_states = at_small + 128
     small_cols = jnp.concatenate(
         [
             mamba_step,
@@ -218,20 +244,23 @@
         ],
         axis=1,
     )
-    mixer_shard = jnp.concatenate(
-        [mamba_gate, mamba_inner, query_weight, keyval_weight, small_cols, mamba_states], axis=1
-    )
-    later_shard = jnp.concatenate(
-        [gate_weight, up_weight, down_weight.T, attention_output.T, mamba_output.T], axis=1
-    )
-    mixer_w = lax.all_gather(mixer_shard, both, axis=0, tiled=True)
-    mixer_w, later_shard = lax.optimization_barrier((mixer_w, later_shard))
-    later_w = lax.all_gather(later_shard, both, axis=0, tiled=True)
-    gate_up = later_w[:, : 2 * ff_w]
-    down_t = later_w[:, 2 * ff_w : 3 * ff_w]
-    out_t = later_w[:, 3 * ff_w :]
-    small_w = mixer_w[:, at_small:at_states]
-    states_w = mixer_w[:, at_states:]
+    first_shard = jnp.concatenate([mamba_inner, mamba_states, keyval_weight, small_cols], axis=1)
+    next_shard = jnp.concatenate(
+        [attention_output.T, mamba_output.T, mamba_gate, query_weight], axis=1
+    )
+    last_shard = jnp.concatenate([gate_weight, up_weight, down_weight.T], axis=1)
+    first_w = lax.all_gather(first_shard, both, axis=0, tiled=True)
+    first_w, next_shard = lax.optimization_barrier((first_w, next_shard))
+    next_w = lax.all_gather(next_shard, both, axis=0, tiled=True)
+    next_w, last_shard = lax.optimization_barrier((next_w, last_shard))
+    last_w = lax.all_gather(last_shard, both, axis=0, tiled=True)
+    gate_up = last_w[:, : 2 * ff_w]
+    down_t = last_w[:, 2 * ff_w :]
+    at_gate = q_width + inner_w
+    out_t = next_w[:, :at_gate]
+    gate_query_w = next_w[:, at_gate:]
+    small_w = first_w[:, at_small:]
+    states_w = first_w[:, at_states:at_keyval]
     pick = (
         jnp.arange(8, dtype=jnp.int32)[:, None] + head_local
         == jnp.arange(128, dtype=jnp.int32)[None, :]
@@ -257,13 +286,14 @@
     mixer_in = (normed_one * gain_one_f).astype(jnp.bfloat16)
     q_heads = q_width // HEAD_DIM
     score_scale = HEAD_DIM ** (-0.5)
-    lin = jnp.dot(mixer_in, mixer_w, preferred_element_type=jnp.float32)
-    mgate_lin = lin[:, :inner_w]
-    inner_pre = lin[:, inner_w:at_query].astype(jnp.bfloat16)
-    query_lin = lin[:, at_query:at_keyval]
+    lin = jnp.dot(mixer_in, first_w, preferred_element_type=jnp.float32)
+    inner_pre = lin[:, :inner_w].astype(jnp.bfloat16)
+    states_pre = lin[:, at_states:at_keyval].astype(jnp.bfloat16)
     keyval_lin = lin[:, at_keyval:at_small]
     step_raw = lin[:, at_small : at_small + head_local]
-    states_pre = lin[:, at_states:].astype(jnp.bfloat16)
+    lin_two = jnp.dot(mixer_in, gate_query_w, preferred_element_type=jnp.float32)
+    mgate_lin = lin_two[:, :inner_w]
+    query_lin = lin_two[:, inner_w:]
     lead_rows = CONV - 1
     halo = shifted(
         jnp.concatenate(
@@ -387,14 +417,7 @@
     _, dev_decay, dev_state = mamba_fn(
         inner_f, states_f, intersection, step_raw, step_bias, decay_log, skip_gain, zero_carry
     )
-    every_state, every_decay = gather_state(dev_state, dev_decay)
-    carry_in = zero_carry
-    for owner in range(ctx_count - 1):
-        carry_in = jnp.where(
-            owner < ctx_index,
-            every_decay[owner][:, None, None] * carry_in + every_state[owner],
-            carry_in,
-        )
+    carry_in = far_states(dev_state, dev_decay, 1)
     mamba_y, _, _ = mamba_fn(
         inner_f, states_f, intersection, step_raw, step_bias, decay_log, skip_gain, carry_in
     )
@@ -419,18 +442,17 @@
     dupper = (dact * silu_ffn).astype(jnp.bfloat16)
     dgate_upper = jnp.concatenate([dgate, dupper], axis=1)
     dffn_in = tensor_sum(times_transposed(dgate_upper, gate_up))
+    last_grad = jnp.concatenate(
+        [
+            transposed_times(ffn_in, dgate_upper).astype(jnp.bfloat16),
+            transposed_times(cotangent, act_low).astype(jnp.bfloat16),
+        ],
+        axis=1,
+    )
+    last_own = lax.psum_scatter(last_grad, both, scatter_dimension=0, tiled=True)
     grad_gain_two, dresid_norm = norm_back(dffn_in, normed_two, inv_two, gain_two_f)
     dresid = cot_f + dresid_norm
     dmix_low = dresid.astype(jnp.bfloat16)
-    later_grad = jnp.concatenate(
-        [
-            transposed_times(ffn_in, dgate_upper).astype(jnp.bfloat16),
-            transposed_times(cotangent, act_low).astype(jnp.bfloat16),
-            transposed_times(dmix_low, mixed_low).astype(jnp.bfloat16),
-        ],
-        axis=1,
-    )
-    later_own = lax.psum_scatter(later_grad, both, scatter_dimension=0, tiled=True)
     dmixed = jnp.dot(dmix_low, out_t, preferred_element_type=jnp.float32)
     dattn = dmixed[:, :q_width].astype(jnp.bfloat16)
     dgated = dmixed[:, q_width:]
@@ -494,6 +516,16 @@
     dmgate = (dgated * mamba_y * sig_mgate * (1.0 + mgate_lin * (1.0 - sig_mgate))).astype(
         jnp.bfloat16
     )
+    dgate_query = jnp.concatenate([dmgate, dq_lin], axis=1)
+    next_grad = jnp.concatenate(
+        [
+            transposed_times(dmix_low, mixed_low).astype(jnp.bfloat16),
+            transposed_times(mixer_in, dgate_query).astype(jnp.bfloat16),
+        ],
+        axis=1,
+    )
+    next_grad, last_own = lax.optimization_barrier((next_grad, last_own))
+    next_own = lax.psum_scatter(next_grad, both, scatter_dimension=0, tiled=True)
     _, pull_carry = jax.vjp(
         lambda carry_arg: mamba_fn(
             inner_f, states_f, intersection, step_raw, step_bias, decay_log, skip_gain, carry_arg
@@ -501,16 +533,7 @@
         carry_in,
     )
     direct = pull_carry(dmamba_y)[0]
-    every_direct = lax.all_gather(direct.astype(jnp.bfloat16), "ctx", axis=0, tiled=False).astype(
-        jnp.float32
-    )
-    adjoint_next = zero_carry
-    for owner in range(ctx_count - 1, 0, -1):
-        adjoint_next = jnp.where(
-            owner > ctx_index,
-            every_decay[owner][:, None, None] * adjoint_next + every_direct[owner],
-            adjoint_next,
-        )
+    adjoint_next = far_states(direct, dev_decay, -1)
     _, pull_all = jax.vjp(
         mamba_fn,
         inner_f,
@@ -572,13 +595,16 @@
     mine = tp_index == 0
     dstates_half = jnp.where(mine, dstates_low[:, :STATE], dstates_low[:, STATE:])
     states_half = jnp.where(mine, states_w[:, :STATE], states_w[:, STATE:])
-    dlin = jnp.concatenate([dmgate, dinner_low, dq_lin, dkv_lin, dstates_half], axis=1)
-    back_w = jnp.concatenate([mixer_w[:, :at_small], states_half], axis=1)
-    mixer_grad = transposed_times(mixer_in, dlin).astype(jnp.bfloat16)
-    mixer_own = lax.psum_scatter(mixer_grad, both, scatter_dimension=0, tiled=True)
+    dlin = jnp.concatenate([dinner_low, dstates_half, dkv_lin], axis=1)
+    back_w = jnp.concatenate([first_w[:, :inner_w], states_half, first_w[:, at_keyval:at_small]], axis=1)
+    first_grad = transposed_times(mixer_in, dlin).astype(jnp.bfloat16)
+    first_grad, next_own = lax.optimization_barrier((first_grad, next_own))
+    first_own = lax.psum_scatter(first_grad, both, scatter_dimension=0, tiled=True)
     grad_step_t = transposed_times(dstep_low, mixer_in)
     dmixer_in = tensor_sum(
-        times_transposed(dlin, back_w) + times_transposed(dstep_low, small_w[:, :head_local])
+        times_transposed(dgate_query, gate_query_w)
+        + times_transposed(dlin, back_w)
+        + times_transposed(dstep_low, small_w[:, :head_local])
     )
     grad_gain_one, dhidden_norm = norm_back(dmixer_in, normed_one, inv_one, gain_one_f)
     grad_input = dresid + dhidden_norm
@@ -600,7 +626,7 @@
         axis=0,
     )
     spare = -small.shape[0] % 8
-    small = lax.psum(jnp.pad(small, ((0, spare), (0, 0))), both)
+    small = doubling_sum(doubling_sum(jnp.pad(small, ((0, spare), (0, 0))), "shard"), "ctx")
     own_begin = (lax.axis_index("shard") * ctx_count + ctx_index) * shard_rows
     own_cols = lax.dynamic_slice_in_dim(small[: head_local + 2], own_begin, shard_rows, 1)
     base = head_local + 2
@@ -610,32 +636,33 @@
     csbias_row = small[base + CONV + 2, : 2 * STATE]
     heads_row = small[base + CONV + 3]
 
-    later_own = later_own.astype(jnp.float32)
-    at_out = 3 * ff_w
-    states_own = mixer_own[:, at_small : at_small + STATE]
+    at_kv = inner_w + STATE
+    states_own = first_own[:, inner_w:at_kv]
     states_other = lax.ppermute(states_own, "tp", [(0, 1), (1, 0)])
     grad_states = jnp.where(
         mine,
         jnp.concatenate([states_own, states_other], axis=1),
         jnp.concatenate([states_other, states_own], axis=1),
     ).astype(jnp.float32)
-    mixer_own = mixer_own.astype(jnp.float32)
+    first_own = first_own.astype(jnp.float32)
+    next_own = next_own.astype(jnp.float32)
+    last_own = last_own.astype(jnp.float32)
     return (
         output,
         grad_input,
         own_cols[head_local],
         own_cols[head_local + 1],
-        mixer_own[:, :inner_w],
-        mixer_own[:, inner_w:at_query],
+        next_own[:, at_gate : at_gate + inner_w],
+        first_own[:, :inner_w],
         own_cols[:head_local].T,
         grad_states,
-        mixer_own[:, at_query:at_keyval],
-        mixer_own[:, at_keyval:at_small],
-        later_own[:, at_out + q_width :].T,
-        later_own[:, at_out : at_out + q_width].T,
-        later_own[:, :ff_w],
-        later_own[:, ff_w : 2 * ff_w],
-        later_own[:, 2 * ff_w : at_out].T,
+        next_own[:, at_gate + inner_w :],
+        first_own[:, at_kv:],
+        next_own[:, q_width:at_gate].T,
+        next_own[:, :q_width].T,
+        last_own[:, :ff_w],
+        last_own[:, ff_w : 2 * ff_w],
+        last_own[:, 2 * ff_w :].T,
         heads_row[:head_local],
         heads_row[head_local : 2 * head_local],
         heads_row[2 * head_local : 3 * head_local],

time: 883 us -> 728 us (0.82)
  blocking collectives: 88 us -> 0 us
  waiting for transfers between devices: 437 us -> 370 us
  starting transfers between devices: 17.2 us -> 46.2 us
  other arithmetic: 119 us -> 105 us
  local copies, waits for them, and re-layouts: 92.1 us -> 80.6 us
    reduce_scatter x2, waiting for transfers between devices: 267 us -> 134 us  [the longest x1 98 us: local(): lax.psum_scatter(last_grad, both, scatter_dimension=0, tiled=True)]
    all_gather x2 -> x0, blocking collectives: 88 us -> none  [the longest x1 70.4 us: gather_state(): lax.all_gather(packed, 'ctx', axis=0, tiled=False).astype(jnp.float32)]
    psum x1 -> x0, waiting for transfers between devices: 84.5 us -> none  [local(): small = lax.psum(jnp.pad(small, ((0, spare), (0, 0))), both)]
    ppermute x8 -> x14, waiting for transfers between devices: 11.3 us -> 93.4 us  [shifted(): return lax.ppermute(block, axis, route)]
    all_gather x2 -> x3, waiting for transfers between devices: 72.1 us -> 118 us  [the longest x1 65.1 us: local(): first_w = lax.all_gather(first_shard, both, axis=0, tiled=True)]
    ppermute x8 -> x14, starting transfers between devices: 15.7 us -> 41.2 us  [shifted(): return lax.ppermute(block, axis, route)]
    ppermute x0 -> x4, waiting for transfers between devices: none -> 22.1 us  [doubling_sum(): lax.ppermute(values, axis, [(i, i ^ step) for i in range(count)])]
    unnamed x372 -> x380, local copies, waits for them, and re-layouts: 16.8 us -> 27.7 us
  transfers between devices with their start and end apart: 19 -> 30, of which waited for: 6 -> 17; matrix products, arithmetic and copies ran while one was open for 21% -> 35% of each run, Pallas kernels for 0% -> 0%
where the time goes in v2:
time: 728 us; the launch traced here: 718 us
  waiting for transfers between devices  370 us (51%)
  other arithmetic  105 us (14%)
  matrix products  97.3 us (13%)
  local copies, waits for them, and re-layouts  80.6 us (11%)
  starting transfers between devices  46.2 us (6%)
  between operations  18 us (2%)
    reduce_scatter x1, waiting for transfers between devices, local(): lax.psum_scatter(last_grad, both, scatter_dimension=0, tiled=True)  98 us
    ppermute x14, waiting for transfers between devices, shifted(): return lax.ppermute(block, axis, route)  93.4 us
    all_gather x1, waiting for transfers between devices, local(): first_w = lax.all_gather(first_shard, both, axis=0, tiled=True)  65.1 us
    all_gather x1, waiting for transfers between devices, local(): next_w = lax.all_gather(next_shard, both, axis=0, tiled=True)  49.4 us
    ppermute x14, starting transfers between devices, shifted(): return lax.ppermute(block, axis, route)  41.2 us
    reduce_scatter x1, waiting for transfers between devices, local(): lax.psum_scatter(first_grad, both, scatter_dimension=0, tiled=True)  35.8 us
    unnamed x380, local copies, waits for them, and re-layouts  27.7 us
    ppermute x4, waiting for transfers between devices, doubling_sum(): lax.ppermute(values, axis, [(i, i ^ step) for i in range(count)])  22.1 us
  transfers between devices with their start and end apart: 30, of which 17 were waited for; matrix products, arithmetic and copies ran while one was open for 35% of the time, Pallas kernels for 0%

profile of v2, /device:TPU:0, one launch (start us, length us, event | category | flops | bytes accessed | tf_op | source)
XLA Modules:
  0.0 717.7 jit_solution(16532959025811892534)
XLA Ops:
  13.2 65.1 %all-gather.4.cloned.1.call-done = bf16[1024,1280]{1,0:T(8,128)(2,1)} async-done(((bf16[64,1280]{1,0:T(8,128)(2,1)}), bf16[1024,1280]{1,0:T(8,128)(2,1)}) %all-gather.4.cloned.1.call-update) | async-done | bytes 2621456 | tf_op jit(solution)/shard_map/all_gather | solution.py:252
  88.9 2.1 and_and_fusion
  92.2 4.8 fusion.259
  97.0 3.2 copy.565
  103.0 1.9 convert.79
  107.3 49.4 %all-gather.6.cloned.1.call-done = bf16[1024,2048]{1,0:T(8,128)(2,1)} async-done(((bf16[64,2048]{1,0:T(8,128)(2,1)}), bf16[1024,2048]{1,0:T(8,128)(2,1)}) %all-gather.6.cloned.1.call-update) | async-done | bytes 4194320 | tf_op jit(solution)/shard_map/all_gather | solution.py:254
  157.4 4.5 collective-permute-start.2
  161.9 1.9 collective-permute-start.1
  163.8 2.5 collective-permute-start
  170.8 13.2 %collective-permute-done.3 = bf16[3,1024]{0,1:T(8,128)(2,1)S(1)} collective-permute-done((bf16[3,1024]{0,1:T(8,128)(2,1)S(1)}, bf16[3,1024]{0,1:T(8,128)(2,1)S(1)}, u32[]{:S(2)}, u32[]{:S(2)}) %collective-permute-start.3) | collective-permute-done | bytes 6176 | tf_op jit(solution)/shard_map/ppermute | solution.py:20
  188.6 2.9 multiply_convert_fusion.5
  196.0 6.9 collective-permute-start.6
  202.9 3.3 collective-permute-start.5
  206.2 2.1 reshape.875
  209.7 10.9 %collective-permute-start.4 = (bf16[12,136,64]{1,2,0:T(8,128)(2,1)}, bf16[12,136,64]{1,2,0:T(8,128)(2,1)S(1)}, u32[]{:S(2)}, u32[]{:S(2)}) collective-permute-start(bf16[12,136,64]{1,2,0:T(8,128)(2,1)} %pad_maximum_fusion.17), channel_id=1, source_target_pairs={{0,2},{2,4},{4,6},{1,3},{3,5},{5,7},{8,10},{10,12},{12,14},{9,11},... | collective-permute-start | bytes 626696 | tf_op jit(solution)/shard_map/ppermute | solution.py:20
  223.6 2.4 collective-permute-done.5
  227.0 6.8 collective-permute-done.4
  238.0 2.0 fusion.84
  245.7 3.1 copy.654
  250.1 4.5 select_reduce_fusion
  254.7 5.0 fusion.1
  261.1 5.6 fusion.275
  268.1 2.6 collective-permute-done.7
  271.3 3.5 all-gather.8.cloned.1.call-done
  274.8 4.7 fusion.18
  279.5 3.5 fusion.57
  284.7 2.5 convolution_convert_fusion
  287.1 3.2 pad_maximum_fusion
  291.2 6.3 fusion.98
  297.5 3.9 fusion.91
  305.0 3.0 multiply_reduce_fusion.1
  308.0 4.7 multiply_add_fusion
  316.0 3.3 copy.655
  319.3 5.1 multiply_reduce_fusion.5
  324.4 2.3 reshape.878
  336.1 9.2 %multiply_convert_fusion = bf16[512,4,2048]{2,0,1:T(8,128)(2,1)S(1)} fusion(f32[512,4,2048]{2,0,1:T(8,128)} %copy-done.4, f32[512,4]{0,1:T(4,128)S(1)} %multiply_reduce_fusion.9, f32[512,4]{0,1:T(4,128)} %get-tuple-element.350, pred[512,2048]{1,0:T(8,128)(4,1)} %and_and_fusion, bf16[512,4,64]{0,2,1:T(8,128)(2,1)} %bitcast.303, ...), kind=kOutput, calls=%fused_computation | convolution fusion | flops 562036736 | bytes 26755072 | tf_op jit(solution)/shard_map/qhd,kd->qhk/dot_general | solution.py:475
  345.4 2.7 convolution_multiply_fusion
  349.9 8.1 %fusion.38 = f32[2048,64]{0,1:T(8,128)S(1)} fusion(bf16[512,4,64]{0,2,1:T(8,128)(2,1)S(1)} %bitcast.304, f32[512,4,2048]{2,0,1:T(8,128)} %copy-done.4, f32[512,4]{0,1:T(4,128)S(1)} %copy-done.148, pred[512,2048]{1,0:T(8,128)(4,1)S(1)} %copy-done.30), kind=kOutput, calls=%fused_computation.52 | convolution fusion | flops 553648128 | bytes 18620416 | tf_op jit(solution)/shard_map/qhk,qhd->kd/dot_general | solution.py:489
  359.0 5.8 fusion.21
  371.1 2.6 pad_maximum_fusion.1
  374.8 2.8 fusion.70
  377.6 98.0 %reduce-scatter.6.cloned.1.call-done = bf16[64,3072]{1,0:T(8,128)(2,1)} async-done(((bf16[1024,3072]{1,0:T(8,128)(2,1)}), bf16[64,3072]{1,0:T(8,128)(2,1)}) %reduce-scatter.6.cloned.1.call-update) | async-done | bytes 393232 | tf_op jit(solution)/shard_map/reduce_scatter | solution.py:452
  475.6 6.5 copy.651
  495.2 2.4 multiply_reduce_fusion.7
  497.6 5.8 collective-permute-done.15
  505.0 9.6 %collective-permute-done.16 = bf16[512,128]{0,1:T(8,128)(2,1)} collective-permute-done((bf16[512,128]{0,1:T(8,128)(2,1)S(1)}, bf16[512,128]{0,1:T(8,128)(2,1)}, u32[]{:S(2)}, u32[]{:S(2)}) %collective-permute-start.16) | collective-permute-done | bytes 131104 | tf_op jit(solution)/shard_map/ppermute | solution.py:20
  519.5 14.3 %collective-permute-done.10 = bf16[12,136,64]{1,2,0:T(8,128)(2,1)S(1)} collective-permute-done((bf16[12,136,64]{1,2,0:T(8,128)(2,1)}, bf16[12,136,64]{1,2,0:T(8,128)(2,1)S(1)}, u32[]{:S(2)}, u32[]{:S(2)}) %collective-permute-start.10) | collective-permute-done | bytes 208928 | tf_op jit(solution)/shard_map/ppermute | solution.py:20
  541.8 2.0 fusion.83
  548.4 5.0 reduce-window.21
  554.0 2.5 add_multiply_fusion
  560.2 41.4 %collective-permute-done.13 = f32[3,1024]{0,1:T(8,128)S(1)} collective-permute-done((f32[3,1024]{0,1:T(8,128)S(1)}, f32[3,1024]{0,1:T(8,128)S(1)}, u32[]{:S(2)}, u32[]{:S(2)}) %collective-permute-start.13) | collective-permute-done | bytes 12320 | tf_op jit(solution)/shard_map/ppermute | solution.py:20
  609.5 2.0 fusion.81
  612.9 2.6 fusion.49
  615.6 2.8 convolution_convert_fusion.3
  618.3 2.0 copy.652
  620.4 3.9 add_convert_fusion
  625.9 3.2 fusion.78
  631.3 2.5 fusion.47
  635.5 4.2 collective-permute-done.19
  641.3 4.9 collective-permute-done.20
  646.3 6.9 collective-permute-done.21
  653.2 3.6 fusion.46
  656.9 6.2 collective-permute-done.22
  669.0 35.8 %reduce-scatter.8.cloned.1.call-done = bf16[64,1024]{1,0:T(8,128)(2,1)} async-done(((bf16[1024,1024]{1,0:T(8,128)(2,1)}), bf16[64,1024]{1,0:T(8,128)(2,1)}) %reduce-scatter.8.cloned.1.call-update) | async-done | bytes 131088 | tf_op jit(solution)/shard_map/reduce_scatter | solution.py:602
  (667 shorter events, 148.1 us)
Async XLA Ops:
  7.2 79.5 %copy-start.5 = (bf16[512,1024]{1,0:T(8,128)(2,1)S(1)}, bf16[512,1024]{1,0:T(8,128)(2,1)}, u32[]{:S(2)}) copy-start(bf16[512,1024]{1,0:T(8,128)(2,1)} %param.23) | copy-start | bytes 3145732
  7.2 79.8 %copy-start.176 = (f32[12]{0:T(128)S(1)}, f32[12]{0:T(128)}, u32[]{:S(2)}) copy-start(f32[12]{0:T(128)} %param.39) | copy-start | bytes 148
  7.2 79.8 %copy-start.149 = (bf16[4,256]{1,0:T(4,128)(2,1)S(1)}, bf16[4,256]{1,0:T(4,128)(2,1)}, u32[]{:S(2)}) copy-start(bf16[4,256]{1,0:T(4,128)(2,1)} %param.44) | copy-start | bytes 6148
  7.2 80.9 %copy-start.94 = (bf16[1024,64]{0,1:T(8,128)(2,1)S(1)}, bf16[1024,64]{0,1:T(8,128)(2,1)}, u32[]{:S(2)}) copy-start(bf16[1024,64]{0,1:T(8,128)(2,1)} %param.38) | copy-start | bytes 393220
  7.2 80.9 %copy-start.95 = (bf16[64,1024]{1,0:T(8,128)(2,1)S(1)}, bf16[64,1024]{1,0:T(8,128)(2,1)}, u32[]{:S(2)}) copy-start(bf16[64,1024]{1,0:T(8,128)(2,1)} %param.37) | copy-start | bytes 393220
  7.2 80.9 %copy-start.96 = (bf16[64,1024]{1,0:T(8,128)(2,1)S(1)}, bf16[64,1024]{1,0:T(8,128)(2,1)}, u32[]{:S(2)}) copy-start(bf16[64,1024]{1,0:T(8,128)(2,1)} %param.36) | copy-start | bytes 393220
  7.3 71.0 %all-gather.4.cloned.1.call-start = ((), (), s32[]{:S(2)}) async-start(), calls=%async_computation.3 | async-start | bytes 2785280 | tf_op jit(solution)/shard_map/all_gather | solution.py:252
  11.4 145.3 %all-gather.6.cloned.1.call-start = ((), (), s32[]{:S(2)}) async-start(), calls=%async_computation.4 | async-start | bytes 4456448 | tf_op jit(solution)/shard_map/all_gather | solution.py:254
  78.3 196.5 %all-gather.8.cloned.1.call-start = ((), (), s32[]{:S(2)}) async-start(), calls=%async_computation.5 | async-start | bytes 6684672 | tf_op jit(solution)/shard_map/all_gather | solution.py:256
  82.9 23.3 %copy-start.116 = (f32[512]{0:T(512)}, f32[512]{0:T(512)S(1)}, u32[]{:S(2)}) copy-start(f32[512]{0:T(512)S(1)} %get-tuple-element.295) | copy-start | bytes 6148
  83.7 22.8 %copy-start.150 = (f32[2]{0:T(128)}, f32[2]{0:T(128)S(1)}, u32[]{:S(2)}) copy-start(f32[2]{0:T(128)S(1)} %compare_convert_fusion.3) | copy-start | bytes 28
  85.0 21.2 %copy-start.152 = (f32[32]{0:T(128)}, f32[32]{0:T(128)S(1)}, u32[]{:S(2)}) copy-start(f32[32]{0:T(128)S(1)} %multiply_power_fusion) | copy-start | bytes 388
  85.9 102.6 %copy-start.102 = (f32[768]{0:T(1024)}, f32[768]{0:T(1024)S(1)}, u32[]{:S(2)}) copy-start(f32[768]{0:T(1024)S(1)} %get-tuple-element.280) | copy-start | bytes 9220
  85.9 102.6 %copy-start.104 = (f32[768]{0:T(1024)}, f32[768]{0:T(1024)S(1)}, u32[]{:S(2)}) copy-start(f32[768]{0:T(1024)S(1)} %get-tuple-element.281) | copy-start | bytes 9220
  85.9 102.6 %copy-start.106 = (f32[768]{0:T(1024)}, f32[768]{0:T(1024)S(1)}, u32[]{:S(2)}) copy-start(f32[768]{0:T(1024)S(1)} %get-tuple-element.282) | copy-start | bytes 9220
  85.9 102.6 %copy-start.108 = (f32[768]{0:T(1024)}, f32[768]{0:T(1024)S(1)}, u32[]{:S(2)}) copy-start(f32[768]{0:T(1024)S(1)} %get-tuple-element.283) | copy-start | bytes 9220
  87.1 154.3 %copy-start.125 = (f32[512]{0:T(512)}, f32[512]{0:T(512)S(1)}, u32[]{:S(2)}) copy-start(f32[512]{0:T(512)S(1)} %add_rsqrt_fusion.1) | copy-start | bytes 6148
  87.1 97.0 %copy-start.140 = (f32[1,256]{1,0:T(1,128)}, f32[1,256]{1,0:T(1,128)S(1)}, u32[]{:S(2)}) copy-start(f32[1,256]{1,0:T(1,128)S(1)} %get-tuple-element.367) | copy-start | bytes 3076
  87.1 97.0 %copy-start.142 = (f32[1,256]{1,0:T(1,128)}, f32[1,256]{1,0:T(1,128)S(1)}, u32[]{:S(2)}) copy-start(f32[1,256]{1,0:T(1,128)S(1)} %get-tuple-element.368) | copy-start | bytes 3076
  87.1 97.0 %copy-start.144 = (f32[1,256]{1,0:T(1,128)}, f32[1,256]{1,0:T(1,128)S(1)}, u32[]{:S(2)}) copy-start(f32[1,256]{1,0:T(1,128)S(1)} %get-tuple-element.369) | copy-start | bytes 3076
  87.1 97.0 %copy-start.146 = (f32[1,256]{1,0:T(1,128)}, f32[1,256]{1,0:T(1,128)S(1)}, u32[]{:S(2)}) copy-start(f32[1,256]{1,0:T(1,128)S(1)} %get-tuple-element.370) | copy-start | bytes 3076
  92.2 149.2 %copy-start.111 = (f32[1,1024]{1,0:T(1,128)}, f32[1,1024]{1,0:T(1,128)S(1)}, u32[]{:S(2)}) copy-start(f32[1,1024]{1,0:T(1,128)S(1)} %get-tuple-element.347) | copy-start | bytes 12292
  101.3 65.3 %copy-start.40 = (f32[512,12]{1,0:T(8,128)}, f32[512,12]{1,0:T(8,128)S(1)}, u32[]{:S(2)}) copy-start(f32[512,12]{1,0:T(8,128)S(1)} %get-tuple-element.302) | copy-start | bytes 73732
  103.0 66.5 %copy-start.59 = (f32[2,12,256]{2,1,0:T(8,128)}, f32[2,12,256]{2,1,0:T(8,128)S(1)}, u32[]{:S(2)}) copy-start(f32[2,12,256]{2,1,0:T(8,128)S(1)} %reshape.903) | copy-start | bytes 73732
  105.0 65.8 %copy-start.25 = (bf16[512,1280]{0,1:T(8,128)(2,1)}, bf16[512,1280]{0,1:T(8,128)(2,1)S(1)}, u32[]{:S(2)}) copy-start(bf16[512,1280]{0,1:T(8,128)(2,1)S(1)} %convert.79) | copy-start | bytes 3932164
  105.0 65.8 %copy-start.69 = (bf16[512,64]{0,1:T(8,128)(2,1)}, bf16[512,64]{0,1:T(8,128)(2,1)S(1)}, u32[]{:S(2)}) copy-start(bf16[512,64]{0,1:T(8,128)(2,1)S(1)} %slice.644) | copy-start | bytes 196612
  105.2 65.6 %copy-start.114 = (f32[2,12]{1,0:T(2,128)}, f32[2,12]{1,0:T(2,128)S(1)}, u32[]{:S(2)}) copy-start(f32[2,12]{1,0:T(2,128)S(1)} %slice_reduce_fusion.2) | copy-start | bytes 292
  106.6 77.5 %copy-start.70 = (bf16[512,64]{0,1:T(8,128)(2,1)}, bf16[512,64]{0,1:T(8,128)(2,1)S(1)}, u32[]{:S(2)}) copy-start(bf16[512,64]{0,1:T(8,128)(2,1)S(1)} %maximum_bitcast_fusion) | copy-start | bytes 196612
  156.7 318.9 %reduce-scatter.6.cloned.1.call-start = ((), (), s32[]{:S(2)}) async-start(), calls=%async_computation.6 | async-start | bytes 6684672 | tf_op jit(solution)/shard_map/reduce_scatter | solution.py:452
  157.4 52.3 %collective-permute-start.2 = (bf16[512,128]{0,1:T(8,128)(2,1)}, bf16[512,128]{0,1:T(8,128)(2,1)}, u32[]{:S(2)}, u32[]{:S(2)}) collective-permute-start(bf16[512,128]{0,1:T(8,128)(2,1)} %pad_maximum_fusion.28), channel_id=1, source_target_pairs={{0,6},{1,7},{8,14},{9,15},{16,22},{17,23},{24,30},{25,31}} | collective-permute-start | bytes 393224 | tf_op jit(solution)/shard_map/ppermute | solution.py:20
  161.9 58.7 %collective-permute-start.1 = (bf16[512,128]{0,1:T(8,128)(2,1)}, bf16[512,128]{0,1:T(8,128)(2,1)}, u32[]{:S(2)}, u32[]{:S(2)}) collective-permute-start(bf16[512,128]{0,1:T(8,128)(2,1)} %pad_maximum_fusion.28), channel_id=1, source_target_pairs={{0,4},{2,6},{1,5},{3,7},{8,12},{10,14},{9,13},{11,15},{16,20},{18,... | collective-permute-start | bytes 393224 | tf_op jit(solution)/shard_map/ppermute | solution.py:20
  163.8 56.8 %collective-permute-start = (bf16[512,128]{0,1:T(8,128)(2,1)}, bf16[512,128]{0,1:T(8,128)(2,1)}, u32[]{:S(2)}, u32[]{:S(2)}) collective-permute-start(bf16[512,128]{0,1:T(8,128)(2,1)} %pad_maximum_fusion.28), channel_id=1, source_target_pairs={{0,2},{2,4},{4,6},{1,3},{3,5},{5,7},{8,10},{10,12},{12,14},{9,11},... | collective-permute-start | bytes 393224 | tf_op jit(solution)/shard_map/ppermute | solution.py:20
  166.8 17.1 %collective-permute-start.3 = (bf16[3,1024]{0,1:T(8,128)(2,1)S(1)}, bf16[3,1024]{0,1:T(8,128)(2,1)S(1)}, u32[]{:S(2)}, u32[]{:S(2)}) collective-permute-start(bf16[3,1024]{0,1:T(8,128)(2,1)S(1)} %slice.651), channel_id=1, source_target_pairs={{0,2},{2,4},{4,6},{1,3},{3,5},{5,7},{8,10},{10,12},{12,14},{9,11},... | collective-permute-start | bytes 18440 | tf_op jit(solution)/shard_map/ppermute | solution.py:20
  191.7 46.2 %copy-start.34 = (bf16[2,256,12,64]{1,0,3,2:T(2,128)(2,1)}, bf16[2,256,12,64]{1,0,3,2:T(2,128)(2,1)S(1)}, u32[]{:S(2)}) copy-start(bf16[2,256,12,64]{1,0,3,2:T(2,128)(2,1)S(1)} %reshape.873) | copy-start | bytes 2359300
  192.9 41.9 %copy-start.38 = (f32[2,12,128,64]{2,3,1,0:T(8,128)}, f32[2,12,128,64]{2,3,1,0:T(8,128)S(1)}, u32[]{:S(2)}) copy-start(f32[2,12,128,64]{2,3,1,0:T(8,128)S(1)} %fusion.111) | copy-start | bytes 2359300
  196.0 26.5 %collective-permute-start.6 = (bf16[12,136,64]{1,2,0:T(8,128)(2,1)}, bf16[12,136,64]{1,2,0:T(8,128)(2,1)}, u32[]{:S(2)}, u32[]{:S(2)}) collective-permute-start(bf16[12,136,64]{1,2,0:T(8,128)(2,1)} %pad_maximum_fusion.17), channel_id=1, source_target_pairs={{0,6},{1,7},{8,14},{9,15},{16,22},{17,23},{24,30},{25,31}} | collective-permute-start | bytes 626696 | tf_op jit(solution)/shard_map/ppermute | solution.py:20
  202.9 23.1 %collective-permute-start.5 = (bf16[12,136,64]{1,2,0:T(8,128)(2,1)}, bf16[12,136,64]{1,2,0:T(8,128)(2,1)}, u32[]{:S(2)}, u32[]{:S(2)}) collective-permute-start(bf16[12,136,64]{1,2,0:T(8,128)(2,1)} %pad_maximum_fusion.17), channel_id=1, source_target_pairs={{0,4},{2,6},{1,5},{3,7},{8,12},{10,14},{9,13},{11,15},{16,20},{18,... | collective-permute-start | bytes 626696 | tf_op jit(solution)/shard_map/ppermute | solution.py:20
  209.7 28.3 %copy-start.76 = (f32[2,256,256]{2,1,0:T(8,128)}, f32[2,256,256]{2,1,0:T(8,128)S(1)}, u32[]{:S(2)}) copy-start(f32[2,256,256]{2,1,0:T(8,128)S(1)} %fusion.277) | copy-start | bytes 1572868
  209.7 25.1 %copy-start.136 = (f32[12]{0:T(128)S(1)}, f32[12]{0:T(128)}, u32[]{:S(2)}) copy-start(f32[12]{0:T(128)} %copy-done.135) | copy-start | bytes 148
  209.7 24.2 %collective-permute-start.4 = (bf16[12,136,64]{1,2,0:T(8,128)(2,1)}, bf16[12,136,64]{1,2,0:T(8,128)(2,1)S(1)}, u32[]{:S(2)}, u32[]{:S(2)}) collective-permute-start(bf16[12,136,64]{1,2,0:T(8,128)(2,1)} %pad_maximum_fusion.17), channel_id=1, source_target_pairs={{0,2},{2,4},{4,6},{1,3},{3,5},{5,7},{8,10},{10,12},{12,14},{9,11},... | collective-permute-start | bytes 626696 | tf_op jit(solution)/shard_map/ppermute | solution.py:20
  268.0 2.7 collective-permute-start.7
  290.4 328.0 %reduce-scatter.10.cloned.1.call-start = ((), (), s32[]{:S(2)}) async-start(), calls=%async_computation.8 | async-start | bytes 4456448
  297.5 7.6 %collective-permute-start.9 = (bf16[512,1024]{1,0:T(8,128)(2,1)}, bf16[512,1024]{1,0:T(8,128)(2,1)}, u32[]{:S(2)}, u32[]{:S(2)}) collective-permute-start(bf16[512,1024]{1,0:T(8,128)(2,1)} %fusion.98), channel_id=1, source_target_pairs={{0,1},{1,0},{2,3},{3,2},{4,5},{5,4},{6,7},{7,6},{8,9},{9,8},{10,11... | collective-permute-start | bytes 3145736 | tf_op jit(solution)/shard_map/ppermute | solution.py:161
  301.4 6.7 collective-permute-start.8
  330.3 187.1 %collective-permute-start.12 = (bf16[12,136,64]{1,2,0:T(8,128)(2,1)}, bf16[12,136,64]{1,2,0:T(8,128)(2,1)}, u32[]{:S(2)}, u32[]{:S(2)}) collective-permute-start(bf16[12,136,64]{1,2,0:T(8,128)(2,1)} %pad_maximum_fusion.16), channel_id=1, source_target_pairs={{6,0},{7,1},{14,8},{15,9},{22,16},{23,17},{30,24},{31,25}} | collective-permute-start | bytes 626696 | tf_op jit(solution)/shard_map/ppermute | solution.py:20
  331.6 186.9 %collective-permute-start.11 = (bf16[12,136,64]{1,2,0:T(8,128)(2,1)}, bf16[12,136,64]{1,2,0:T(8,128)(2,1)}, u32[]{:S(2)}, u32[]{:S(2)}) collective-permute-start(bf16[12,136,64]{1,2,0:T(8,128)(2,1)} %pad_maximum_fusion.16), channel_id=1, source_target_pairs={{4,0},{6,2},{5,1},{7,3},{12,8},{14,10},{13,9},{15,11},{20,16},{22,... | collective-permute-start | bytes 626696 | tf_op jit(solution)/shard_map/ppermute | solution.py:20
  482.1 222.7 %reduce-scatter.8.cloned.1.call-start = ((), (), s32[]{:S(2)}) async-start(), calls=%async_computation.7 | async-start | bytes 2228224 | tf_op jit(solution)/shard_map/reduce_scatter | solution.py:602
  485.9 17.4 %collective-permute-start.15 = (bf16[512,128]{0,1:T(8,128)(2,1)}, bf16[512,128]{0,1:T(8,128)(2,1)}, u32[]{:S(2)}, u32[]{:S(2)}) collective-permute-start(bf16[512,128]{0,1:T(8,128)(2,1)} %get-tuple-element.327), channel_id=1, source_target_pairs={{2,0},{4,2},{6,4},{3,1},{5,3},{7,5},{10,8},{12,10},{14,12},{11,9},... | collective-permute-start | bytes 393224 | tf_op jit(solution)/shard_map/ppermute | solution.py:20
  487.2 17.8 %collective-permute-start.17 = (bf16[512,128]{0,1:T(8,128)(2,1)}, bf16[512,128]{0,1:T(8,128)(2,1)}, u32[]{:S(2)}, u32[]{:S(2)}) collective-permute-start(bf16[512,128]{0,1:T(8,128)(2,1)} %get-tuple-element.328), channel_id=1, source_target_pairs={{6,0},{7,1},{14,8},{15,9},{22,16},{23,17},{30,24},{31,25}} | collective-permute-start | bytes 393224 | tf_op jit(solution)/shard_map/ppermute | solution.py:20
  488.5 26.1 %collective-permute-start.16 = (bf16[512,128]{0,1:T(8,128)(2,1)S(1)}, bf16[512,128]{0,1:T(8,128)(2,1)}, u32[]{:S(2)}, u32[]{:S(2)}) collective-permute-start(bf16[512,128]{0,1:T(8,128)(2,1)S(1)} %get-tuple-element.329), channel_id=1, source_target_pairs={{4,0},{6,2},{5,1},{7,3},{12,8},{14,10},{13,9},{15,11},{20,16},{22,... | collective-permute-start | bytes 393224 | tf_op jit(solution)/shard_map/ppermute | solution.py:20
  495.2 20.6 %copy-start.153 = (f32[32]{0:T(128)S(1)}, f32[32]{0:T(128)}, u32[]{:S(2)}) copy-start(f32[32]{0:T(128)} %copy-done.152) | copy-start | bytes 388
  503.3 30.5 %collective-permute-start.10 = (bf16[12,136,64]{1,2,0:T(8,128)(2,1)}, bf16[12,136,64]{1,2,0:T(8,128)(2,1)S(1)}, u32[]{:S(2)}, u32[]{:S(2)}) collective-permute-start(bf16[12,136,64]{1,2,0:T(8,128)(2,1)} %pad_maximum_fusion.16), channel_id=1, source_target_pairs={{2,0},{4,2},{6,4},{3,1},{5,3},{7,5},{10,8},{12,10},{14,12},{11,9},... | collective-permute-start | bytes 626696 | tf_op jit(solution)/shard_map/ppermute | solution.py:20
  556.6 45.9 %copy-start.17 = (f32[512,256]{0,1:T(8,128)S(1)}, f32[512,256]{0,1:T(8,128)}, u32[]{:S(2)}) copy-start(f32[512,256]{0,1:T(8,128)} %copy-done.16) | copy-start | bytes 1572868
  556.6 45.9 %copy-start.110 = (f32[515]{0:T(1024)S(1)}, f32[515]{0:T(1024)}, u32[]{:S(2)}) copy-start(f32[515]{0:T(1024)} %get-tuple-element.358) | copy-start | bytes 6184
  556.7 45.9 %copy-start.3 = (f32[515,256]{0,1:T(8,128)S(1)}, f32[515,256]{0,1:T(8,128)}, u32[]{:S(2)}) copy-start(f32[515,256]{0,1:T(8,128)} %copy-done.2) | copy-start | bytes 1582084
  556.7 44.9 %collective-permute-start.13 = (f32[3,1024]{0,1:T(8,128)S(1)}, f32[3,1024]{0,1:T(8,128)S(1)}, u32[]{:S(2)}, u32[]{:S(2)}) collective-permute-start(f32[3,1024]{0,1:T(8,128)S(1)} %pad_maximum_fusion.19), channel_id=1, source_target_pairs={{2,0},{4,2},{6,4},{3,1},{5,3},{7,5},{10,8},{12,10},{14,12},{11,9},... | collective-permute-start | bytes 36872 | tf_op jit(solution)/shard_map/ppermute | solution.py:20
  607.6 4.3 collective-permute-start.14
  624.3 7.0 collective-permute-start.18
  631.3 22.0 %copy-start.20 = (f32[512,1024]{1,0:T(8,128)S(1)}, f32[512,1024]{1,0:T(8,128)}, u32[]{:S(2)}) copy-start(f32[512,1024]{1,0:T(8,128)} %copy-done.18) | copy-start | bytes 6291460
  634.0 5.7 collective-permute-start.19
  639.7 6.4 collective-permute-start.20
  646.2 7.0 collective-permute-start.21
  653.2 9.9 %collective-permute-start.22 = (f32[24,1024]{1,0:T(8,128)S(1)}, f32[24,1024]{1,0:T(8,128)S(1)}, u32[]{:S(2)}, u32[]{:S(2)}) collective-permute-start(f32[24,1024]{1,0:T(8,128)S(1)} %add.551), channel_id=1, source_target_pairs={{0,4},{2,6},{4,0},{6,2},{1,5},{3,7},{5,1},{7,3},{8,12},{10,14},{12... | collective-permute-start | bytes 294920 | tf_op jit(solution)/shard_map/ppermute | solution.py:198
  705.6 4.5 collective-permute-start.23
  (153 other events, 754.4 us)
Sparse Core Ops, SparseCore 0:
  11.5 66.6 all-gather.3
  81.6 75.0 all-gather.5
  159.6 115.2 all-gather.7
  290.5 185.0 reduce-scatter.5
  482.2 122.9 reduce-scatter.9
  620.4 84.3 reduce-scatter.7
